TPU v7x, 32 devices: a whole 2x2x4 slice. The times are simulated.
32 devices in a mesh: col: 16 (over z, y, core), row: 2 (over x).
Axes of the slice: x: 2, y: 2, z: 4, core: 2. Of those that a mesh axis runs over, the one named last changes fastest.
Arguments:
- diag_blocks: float32 [32, 512, 512], P('col'), may hold values from -1 to 3, as said below
- panel_blocks: float32 [32, 8, 512, 512], P('col', None, 'row'), may hold values from -0.3 to 0.3
- ancestors: int32 [32, 8], P('col'), may hold values from 0 to 15, all different within a row; in each aligned block of 2 rows (0 to 1, 2 to 3, ...) at most 2 rows name the same one
- target_ids: int32 [16], P('col'), may hold values from 0 to 15, each once
- target_tiles: float32 [16, 512, 512], P('col', 'row'), may hold values from -6 to 6
Outputs:
- panel_factor: float32 [32, 8, 512, 512], P('col', None, 'row')
- updated_tiles: float32 [16, 512, 512], P('col', 'row')
Inputs may be any that keep to these rules, and one draw needn't show every extreme that they name: `ancestors`: each row names 8 different target blocks; on the supernodes of one index of col a target block is named at most twice, and exactly twice somewhere; every target block is named. `target_ids`: A permutation of the target blocks. `diag_blocks`: each block is symmetric and positive definite, with smallest eigenvalue 0.05 or more.
All inputs are finite; a program needn't handle non-finite values.
Results may differ from a plain program's by a relative error of at most 0.0029.
Values may be sent and summed in bfloat16 or wider, within the bound.
A program may use at most 128 MiB of HBM per device.

v0:
```python
import jax
import jax.numpy as jnp
from jax import lax
from jax.sharding import PartitionSpec as P


def solve_local(diag_block, panel):
    factor = jnp.linalg.cholesky(diag_block)
    blocks, rows, width = panel.shape
    rhs = jnp.swapaxes(panel.reshape(blocks * rows, width), 0, 1)
    solved = jax.scipy.linalg.solve_triangular(factor, rhs, lower=True)
    return jnp.swapaxes(solved, 0, 1).reshape(blocks, rows, width)


def spread_terms(flat_pos, flat_products, total_targets):
    onehot = (flat_pos[:, None] == jnp.arange(total_targets, dtype=jnp.int32)[None, :]).astype(
        jnp.float32
    )
    return jnp.einsum("cn,cab->nab", onehot, flat_products, precision=lax.Precision.HIGHEST)


def on_device(diag_blocks, panel_blocks, ancestors, target_ids, target_tiles):
    panel_factor = jax.vmap(solve_local)(diag_blocks, panel_blocks)
    rounded = panel_factor.astype(jnp.bfloat16)
    sn_count, anc_count, rows, width = rounded.shape
    all_ids = lax.all_gather(target_ids, "col", axis=0, tiled=True)
    total_targets = all_ids.shape[0]
    matches = ancestors[:, :, None] == all_ids[None, None, :]
    position = jnp.sum(
        jnp.where(matches, jnp.arange(total_targets, dtype=jnp.int32)[None, None, :], 0), axis=2
    )
    products = jnp.einsum(
        "sjaw,sjbw->sjab",
        rounded,
        lax.all_gather(rounded, "row", axis=2, tiled=True),
        preferred_element_type=jnp.float32,
    )
    flat_products = products.reshape(sn_count * anc_count, rows, width)
    flat_pos = position.reshape(-1)
    term = spread_terms(flat_pos, flat_products, total_targets)
    update = lax.psum_scatter(term, "col", scatter_dimension=0, tiled=True)
    return (panel_factor, target_tiles - update)


def solution(mesh):
    in_specs = (
        P("col", None, None),
        P("col", None, "row", None),
        P("col", None),
        P("col"),
        P("col", "row", None),
    )
    out_specs = (P("col", None, "row", None), P("col", "row", None))
    return jax.shard_map(
        on_device, mesh=mesh, in_specs=in_specs, out_specs=out_specs, check_vma=False
    )
```

profile of v0, /device:TPU:0, one launch (start us, length us, event | category | flops | bytes accessed | tf_op | source)
XLA Modules:
  0.0 564.6 jit_solution(12227459995789009420)
XLA Ops:
  7.4 3.0 copy.42
  10.4 2.1 fusion.20
  12.5 1.3 copy-done.2
  13.8 23.5 %custom-call.35 = f32[2,128,128]{2,1,0:T(8,128)S(1)} custom-call(f32[2,128,128]{2,1,0:T(8,128)S(1)} %cholesky.274), custom_call_target="Cholesky" | custom-call | tf_op jit(solution)/shard_map/vmap(jit(cholesky))/cholesky | solution.py:8
  37.3 19.7 %custom-call.36 = f32[2,1,128,128]{2,3,1,0:T(8,128)S(1)} custom-call(f32[2,1,128,128]{3,2,1,0:T(8,128)S(1)} %select_bitcast_fusion.2), custom_call_target="InvertDiagBlocksLowerTriangular" | custom-call | tf_op jit(solution)/shard_map/vmap(jit(cholesky))/cholesky | solution.py:8
  57.0 0.3 cholesky.234
  57.3 1.5 constant_dynamic-update-slice_fusion.3
  58.8 1.5 convolution_subtract_fusion.1
  60.3 23.5 %custom-call.37 = f32[2,128,128]{2,1,0:T(8,128)S(1)} custom-call(f32[2,128,128]{2,1,0:T(8,128)S(1)} %cholesky.278), custom_call_target="Cholesky" | custom-call | tf_op jit(solution)/shard_map/vmap(jit(cholesky))/cholesky | solution.py:8
  83.8 20.0 %custom-call.38 = f32[2,1,128,128]{2,3,1,0:T(8,128)S(1)} custom-call(f32[2,1,128,128]{3,2,1,0:T(8,128)S(1)} %get-tuple-element.33), custom_call_target="InvertDiagBlocksLowerTriangular" | custom-call | tf_op jit(solution)/shard_map/vmap(jit(cholesky))/cholesky | solution.py:8
  103.8 0.4 convolution_dynamic-update-slice_fusion
  104.2 1.6 convolution_subtract_fusion.2
  105.8 23.5 %custom-call.39 = f32[2,128,128]{2,1,0:T(8,128)S(1)} custom-call(f32[2,128,128]{2,1,0:T(8,128)S(1)} %cholesky.283), custom_call_target="Cholesky" | custom-call | tf_op jit(solution)/shard_map/vmap(jit(cholesky))/cholesky | solution.py:8
  129.3 19.7 %custom-call.40 = f32[2,1,128,128]{2,3,1,0:T(8,128)S(1)} custom-call(f32[2,1,128,128]{3,2,1,0:T(8,128)S(1)} %get-tuple-element.31), custom_call_target="InvertDiagBlocksLowerTriangular" | custom-call | tf_op jit(solution)/shard_map/vmap(jit(cholesky))/cholesky | solution.py:8
  149.0 0.3 convolution_dynamic-update-slice_fusion.1
  149.2 1.5 convolution_subtract_fusion.3
  150.8 23.5 %custom-call.41 = f32[2,128,128]{2,1,0:T(8,128)S(1)} custom-call(f32[2,128,128]{2,1,0:T(8,128)S(1)} %convolution_subtract_fusion.3), custom_call_target="Cholesky" | custom-call | tf_op jit(solution)/shard_map/vmap(jit(cholesky))/cholesky | solution.py:8
  174.6 1.8 select_select_fusion
  176.4 14.2 %while.1 = (s32[]{:T(128)}, f32[2,512,512]{2,1,0:T(8,128)}, s32[4,2]{0,1:T(2,128)S(1)}, f32[4,2,128,128]{3,2,0,1:T(8,128)}, s32[]{:T(128)}) while((s32[]{:T(128)}, f32[2,512,512]{2,1,0:T(8,128)}, s32[4,2]{0,1:T(2,128)S(1)}, f32[4,2,128,128]{3,2,0,1:T(8,128)}, s32[]{:T(128)}) %tuple.35), condition=%wide.while_cond, body=%wide.while_body.sunk | while | flops 2 | bytes 263777 | solution.py:11
  176.4 0.5 fusion.53
  177.0 3.0 bitcast_dynamic-update-slice_fusion.2
  180.0 0.5 fusion.53
  180.6 3.0 bitcast_dynamic-update-slice_fusion.2
  183.6 0.5 fusion.53
  184.1 3.0 bitcast_dynamic-update-slice_fusion.2
  187.2 0.5 fusion.53
  187.7 2.9 bitcast_dynamic-update-slice_fusion.2
  190.6 79.4 %custom-call.42 = f32[2,4,128,128]{2,3,1,0:T(8,128)S(1)} custom-call(f32[2,4,128,128]{3,2,1,0:T(8,128)} %bitcast.77), custom_call_target="InvertDiagBlocksLowerTriangular" | custom-call | tf_op jit(solution)/shard_map/vmap(jit(_solve_triangular))/triangular_solve | solution.py:11
  270.0 8.8 %copy.66 = f32[2,2048,512]{1,2,0:T(8,128)} copy(f32[2,2048,512]{2,1,0:T(8,128)} %bitcast.76) | data formatting | bytes 16777216 | tf_op jit(solution)/shard_map/vmap()/reshape | solution.py:10
  278.9 3.5 fusion.18
  282.4 3.8 convolution_subtract_fusion
  286.2 1.9 fusion.32
  288.2 3.3 fusion.12
  291.5 1.9 fusion.30
  293.5 5.2 fusion.15
  298.7 1.9 fusion.29
  300.7 3.7 maximum_bitcast_fusion
  304.4 8.7 %copy.67 = f32[2,2048,512]{2,1,0:T(8,128)} copy(f32[2,2048,512]{1,2,0:T(8,128)} %maximum_bitcast_fusion) | data formatting | bytes 16777216
  313.1 5.9 %convert_element_type.4 = bf16[2,8,256,512]{3,2,1,0:T(8,128)(2,1)} convert(f32[2,8,256,512]{3,2,1,0:T(8,128)} %bitcast.70) | non-fusion elementwise | flops 2097152 | bytes 12582912 | tf_op jit(solution)/shard_map/convert_element_type | solution.py:24
  319.7 0.6 dynamic-slice.4
  320.3 0.8 dynamic-update-slice.23
  321.1 13.7 %all-reduce.1 = s32[16]{0:T(128)S(1)} all-reduce(s32[16]{0:T(128)S(1)} %dynamic-update-slice.23), channel_id=1, replica_groups=mesh['col'=16,'row'=2] {'col'}, use_global_device_ids=true, to_apply=%add.1 | all-reduce | flops 16 | bytes 128
  335.1 90.8 %all-gather.2.cloned.1.call-done = bf16[2,8,512,512]{3,2,1,0:T(8,128)(2,1)} async-done(((bf16[2,8,256,512]{3,2,1,0:T(8,128)(2,1)}), bf16[2,8,512,512]{3,2,1,0:T(8,128)(2,1)}) %all-gather.2.cloned.1.call-update) | async-done | bytes 8388624 | tf_op jit(solution)/shard_map/all_gather | solution.py:35
  425.9 7.0 %fusion.44 = f32[2,8,256,512]{3,2,1,0:T(8,128)S(1)} fusion(bf16[2,8,256,512]{3,2,1,0:T(8,128)(2,1)} %convert_element_type.4, bf16[2,8,512,512]{3,2,1,0:T(8,128)(2,1)} %all-gather.2.cloned.1.call-done), kind=kOutput, calls=%fused_computation.76 | convolution fusion | flops 2147483648 | bytes 20971520 | tf_op jit(solution)/shard_map/sjaw,sjbw->sjab/dot_general | solution.py:32
  432.9 9.3 %fusion = f32[16,256,512]{2,0,1:T(8,128)S(1)} fusion(f32[16,256,512]{2,1,0:T(8,128)S(1)} %bitcast.69, s32[16]{0:T(128)S(1)} %eq.31), kind=kOutput, calls=%fused_computation.3 | convolution fusion | flops 402653440 | bytes 16777280 | tf_op jit(solution)/shard_map/cn,cab->nab/dot_general | solution.py:19
  442.2 8.3 %copy.57 = f32[16,256,512]{2,1,0:T(8,128)} copy(f32[16,256,512]{2,0,1:T(8,128)S(1)} %fusion) | data formatting | bytes 16777216 | tf_op jit(solution)/shard_map/cn,cab->nab/dot_general | solution.py:19
  450.6 104.8 %reduce-scatter.2.cloned.1.call-done = f32[1,256,512]{2,1,0:T(8,128)} async-done(((f32[16,256,512]{2,1,0:T(8,128)}), f32[1,256,512]{2,1,0:T(8,128)}) %reduce-scatter.2.cloned.1.call-update) | async-done | bytes 524304 | tf_op jit(solution)/shard_map/reduce_scatter | solution.py:41
  555.4 1.9 sub.3
  (38 shorter events, 1.3 us)
Async XLA Ops:
  7.2 418.7 %all-gather.2.cloned.1.call-start = ((), (), s32[]{:S(2)}) async-start(), calls=%async_computation.1 | async-start | bytes 12582912 | tf_op jit(solution)/shard_map/all_gather | solution.py:35
  7.4 3.0 copy-start.1
  12.5 1.3 copy-start.2
  282.4 5.8 %copy-start = (f32[2,2048,512]{1,2,0:T(8,128)S(1)}, f32[2,2048,512]{1,2,0:T(8,128)}, u32[]{:S(2)}) copy-start(f32[2,2048,512]{1,2,0:T(8,128)} %copy.66) | copy-start | bytes 25165828
  319.0 0.7 copy-start.5
  319.0 15.8 %copy-start.4 = (s32[2,8]{1,0:T(2,128)S(1)}, s32[2,8]{1,0:T(2,128)}, u32[]{:S(2)}) copy-start(s32[2,8]{1,0:T(2,128)} %param.7) | copy-start | bytes 196
  319.0 236.4 %reduce-scatter.2.cloned.1.call-start = ((), (), s32[]{:S(2)}) async-start(), calls=%async_computation.2 | async-start | bytes 8912896 | tf_op jit(solution)/shard_map/reduce_scatter | solution.py:41
  450.6 104.8 %copy-start.3 = (f32[1,256,512]{2,1,0:T(8,128)S(1)}, f32[1,256,512]{2,1,0:T(8,128)}, u32[]{:S(2)}) copy-start(f32[1,256,512]{2,1,0:T(8,128)} %param.9) | copy-start | bytes 1572868
Sparse Core Ops, SparseCore 0:
  319.2 106.7 all-gather.1
  450.7 104.6 reduce-scatter.1
where the time goes:
time: 574 us; the launch traced here: 565 us
  other arithmetic  249 us (43%)
  waiting for transfers between devices  196 us (34%)
  local copies, waits for them, and re-layouts  46.1 us (8%)
  matrix products  44.8 us (8%)
  between operations  15.4 us (3%)
  blocking collectives  13.7 us (2%)
    another operation x16, other arithmetic, solve_local(): factor = jnp.linalg.cholesky(diag_block)  154 us
    reduce_scatter x1, waiting for transfers between devices, on_device(): update = lax.psum_scatter(term, 'col', scatter_dimension=0, tiled=True)  105 us
    all_gather x1, waiting for transfers between devices, on_device(): lax.all_gather(rounded, 'row', axis=2, tiled=True)  90.8 us
    another operation x4, other arithmetic, solve_local(): solved = jax.scipy.linalg.solve_triangular(factor, rhs, lower=True)  81.3 us
    another operation x7, matrix products, solve_local(): solved = jax.scipy.linalg.solve_triangular(factor, rhs, lower=True)  21.7 us
    unnamed x17, local copies, waits for them, and re-layouts  14.4 us
    another operation x12, local copies, waits for them, and re-layouts  14.2 us
    unnamed x1, blocking collectives  13.7 us
  transfers between devices with their start and end apart: 2, of which 2 were waited for; matrix products, arithmetic and copies ran while one was open for 0% of the time, Pallas kernels for 0%

commit v1 on v0

v1 whole, which is shorter than its diff:
```python
import functools

import jax
import jax.numpy as jnp
from jax import lax
from jax.experimental import pallas as pl
from jax.experimental.pallas import tpu as pltpu
from jax.sharding import PartitionSpec as P

NB = 128
F32 = jnp.float32
BF16 = jnp.bfloat16


def dot_exact(a, b):
    return jnp.dot(a, b, preferred_element_type=F32, precision=lax.Precision.HIGHEST)


def eliminate(blocks, frozen):
    count = len(blocks)
    lane = lax.broadcasted_iota(jnp.int32, (1, NB), 1)
    sub = lax.broadcasted_iota(jnp.int32, (8, NB), 0)
    head = [None] * count
    tail = list(blocks)
    for g in range(NB // 8):
        rows = NB - 8 * g - 8
        cols_head, cols_tail = [], []
        for s in range(count):
            a = tail[s]
            head[s], tail[s] = a[:8], (a[8:] if rows else None)
            cols_head.append(
                [jnp.broadcast_to(head[s][:, 8 * g + m : 8 * g + m + 1], (8, NB)) for m in range(8)]
            )
            cols_tail.append(
                [jnp.broadcast_to(tail[s][:, 8 * g + m : 8 * g + m + 1], (rows, NB)) for m in range(8)]
                if rows
                else None
            )
        for k in range(8):
            at = lane == 8 * g + k
            for s in range(count):
                ch, ct = cols_head[s], cols_tail[s]
                inv = lax.rsqrt(ch[k][k : k + 1, :])
                recip = inv * inv
                row = head[s][k : k + 1, :]
                frozen[s, 8 * g + k : 8 * g + k + 1, :] = jnp.where(at, inv, row * inv)
                step = jnp.where(at, 1.0 + recip, row * recip)
                below = jnp.where(sub > k, ch[k], 0.0)
                head[s] = head[s] - below * step
                if rows:
                    tail[s] = tail[s] - ct[k] * step
                for m in range(k + 1, 8):
                    scale = ch[m][k : k + 1, :] * recip
                    ch[m] = ch[m] - below * scale
                    if rows:
                        ct[m] = ct[m] - ct[k] * scale


def factor_kernel(diag_ref, hi_ref, lo_ref, work, frozen):
    count, width, _ = diag_ref.shape
    work[...] = diag_ref[...]
    lower = lax.broadcasted_iota(jnp.int32, (NB, NB), 0) >= lax.broadcasted_iota(
        jnp.int32, (NB, NB), 1
    )
    lane_block = lax.broadcasted_iota(jnp.int32, (1, width), 1) // NB

    def block_step(b, carry):
        here = pl.ds(pl.multiple_of(b * NB, NB), NB)
        eliminate([work[s, here, here] for s in range(count)], frozen)
        own = lane_block == b
        for s in range(count):
            inverse = jnp.where(lower, frozen[s], 0.0)
            work[s, here, :] = dot_exact(inverse, work[s, here, :])
            work[s, here, here] = inverse

        def trailing(i, carry):
            there = pl.ds(pl.multiple_of(i * NB, NB), NB)
            for s in range(count):
                left = work[s, here, there].T
                old = jnp.where(own, 0.0, work[s, there, :])
                work[s, there, :] = old - dot_exact(left, work[s, here, :])
            return carry

        return lax.fori_loop(b + 1, width // NB, trailing, carry)

    lax.fori_loop(0, width // NB, block_step, 0)
    keep = lax.broadcasted_iota(jnp.int32, (width, width), 0) >= lax.broadcasted_iota(
        jnp.int32, (width, width), 1
    )
    for s in range(count):
        inverse = jnp.where(keep, work[s], 0.0).T
        hi = inverse.astype(BF16)
        hi_ref[s] = hi
        lo_ref[s] = (inverse - hi.astype(F32)).astype(BF16)


def inverse_factors(diag_blocks):
    count, width, _ = diag_blocks.shape
    out = jax.ShapeDtypeStruct((count, width, width), BF16)
    return pl.pallas_call(
        factor_kernel,
        out_shape=(out, out),
        in_specs=[pl.BlockSpec(memory_space=pltpu.VMEM)],
        out_specs=(pl.BlockSpec(memory_space=pltpu.VMEM),) * 2,
        scratch_shapes=[
            pltpu.VMEM((count, width, width), F32),
            pltpu.VMEM((count, NB, NB), F32),
        ],
        compiler_params=pltpu.CompilerParams(vmem_limit_bytes=40 * 2**20),
        cost_estimate=pl.CostEstimate(
            flops=40 * 10**9, bytes_accessed=4 * count * width * width, transcendentals=0
        ),
        name="factor",
    )(diag_blocks)


def dot_nt(a, b):
    return lax.dot_general(a, b, (((1,), (1,)), ((), ())), preferred_element_type=F32)


def place_tile(tile, slot, keep_ref, send_ref):
    half = keep_ref.shape[0]

    @pl.when(slot < half)
    def _():
        keep_ref[slot] = tile(keep_ref[slot])

    @pl.when(slot >= half)
    def _():
        send_ref[slot - half] = tile(send_ref[slot - half])


def panel_kernel(
    slot_ref, mine_ref, panel_ref, other_ref, hi_ref, lo_ref,
    out_ref, same_keep, same_send, cross_keep, cross_send,
):
    s, j = pl.program_id(0), pl.program_id(1)
    blocks, rows, width = panel_ref.shape[1:]
    low = width // 2

    @pl.when((s == 0) & (j == 0))
    def _():
        for ref in (same_keep, same_send, cross_keep, cross_send):
            ref[...] = jnp.zeros_like(ref)

    def times_inverse(lhs, factor):
        left = jnp.dot(lhs[:, :low], factor[:low, :low], preferred_element_type=F32)
        right = jnp.dot(lhs, factor[:, low:], preferred_element_type=F32)
        return jnp.concatenate([left, right], axis=1)

    hi, lo = hi_ref[0], lo_ref[0]
    rhs = panel_ref[0].reshape(blocks * rows, width)
    rhs_hi = rhs.astype(BF16)
    rhs_lo = (rhs - rhs_hi.astype(F32)).astype(BF16)
    solved = times_inverse(rhs_hi, hi) + times_inverse(rhs_lo, hi) + times_inverse(rhs_hi, lo)
    out_ref[0] = solved.reshape(blocks, rows, width)
    rounded = solved.astype(BF16).reshape(blocks, rows, width)
    diagonal = lax.broadcasted_iota(jnp.int32, (rows, rows), 0) == lax.broadcasted_iota(
        jnp.int32, (rows, rows), 1
    )
    extra = lax.broadcasted_iota(jnp.int32, (16, rows), 0)
    for i in range(blocks):
        product = dot_nt(rounded[i], rounded[i])
        sums = jnp.sum(jnp.where(diagonal, product, 0.0), axis=0, keepdims=True)
        product = jnp.where(diagonal, 0.0, product)

        def added(old):
            tail = old[rows:].astype(F32)
            total = jnp.sum(tail, axis=0, keepdims=True) + sums
            top = total.astype(BF16).astype(F32)
            rest = jnp.where(extra == 0, top, jnp.where(extra == 1, total - top, 0.0))
            return jnp.concatenate([old[:rows].astype(F32) + product, rest], axis=0).astype(BF16)

        place_tile(added, slot_ref[s, j * blocks + i], same_keep, same_send)

    @pl.when(s == mine_ref[0])
    def _():
        got = other_ref[...].reshape(blocks * rows, width)
        partner = (times_inverse(got, hi) + times_inverse(got, lo)).astype(BF16)
        partner = partner.reshape(blocks, rows, width)
        for i in range(blocks):
            product = dot_nt(rounded[i], partner[i]).astype(BF16)
            place_tile(lambda old: product, slot_ref[s, j * blocks + i], cross_keep, cross_send)


def panel_products(slot, mine, panel_blocks, other, hi, lo, targets):
    count, blocks, rows, width = panel_blocks.shape
    step = 2 if blocks % 2 == 0 else 1
    steps = blocks // step
    shapes = [(targets // 2, rows + 16, rows)] * 2 + [(targets // 2, rows, rows)] * 2
    whole = [pl.BlockSpec(shape, lambda s, j, slot, mine: (0, 0, 0)) for shape in shapes]
    factor = pl.BlockSpec((1, width, width), lambda s, j, slot, mine: (s, 0, 0))
    panel = pl.BlockSpec((1, step, rows, width), lambda s, j, slot, mine: (s, j, 0, 0))

    def other_at(s, j, slot, mine):
        return (jnp.where(s == mine[0], j, jnp.where(s < mine[0], 0, steps - 1)), 0, 0)

    return pl.pallas_call(
        panel_kernel,
        out_shape=[jax.ShapeDtypeStruct(panel_blocks.shape, F32)]
        + [jax.ShapeDtypeStruct(shape, BF16) for shape in shapes],
        grid_spec=pltpu.PrefetchScalarGridSpec(
            num_scalar_prefetch=2,
            grid=(count, steps),
            in_specs=[panel, pl.BlockSpec((step, rows, width), other_at), factor, factor],
            out_specs=[panel] + whole,
        ),
        compiler_params=pltpu.CompilerParams(
            vmem_limit_bytes=56 * 2**20, dimension_semantics=("arbitrary", "arbitrary")
        ),
        name="panel",
    )(slot, mine, panel_blocks, other, hi, lo)


def packed(value, rows):
    if value.shape[-2] == rows:
        return value.astype(BF16)
    total = value[..., rows : rows + 1, :] + value[..., rows + 1 : rows + 2, :]
    top = lax.reduce_precision(total, 8, 7)
    row = lax.broadcasted_iota(jnp.int32, value.shape, value.ndim - 2)
    value = jnp.where(row == rows, top, jnp.where(row == rows + 1, total - top, value))
    return value.astype(BF16)


def halve_and_add(keep, send, order, columns, rows):
    shape = keep.shape[1:]
    for step, bit in enumerate(order):
        got = lax.ppermute(send, "col", [(c, c ^ (1 << bit)) for c in range(columns)])
        value = keep.astype(F32) + got.astype(F32)
        half = value.shape[0] // 2
        if half:
            keep, send = value[:half], packed(value[half:], rows)
    return value.reshape(shape)


def gathered(slot, panel_blocks, hi, lo, columns):
    count, blocks, rows, width = panel_blocks.shape
    inverse = hi.astype(F32) + lo.astype(F32)
    solved = jnp.einsum("sjaw,swv->sjav", panel_blocks, inverse, precision=lax.Precision.HIGHEST)
    rounded = solved.astype(BF16)
    tiles = jnp.zeros((columns, rows, width), F32)
    for s in range(count):
        full = lax.all_gather(rounded[s], "row", axis=1, tiled=True)
        products = jnp.einsum("jaw,jbw->jab", rounded[s], full, preferred_element_type=F32)
        tiles = tiles.at[slot[s]].add(products)
    return solved, tiles


def on_device(columns, halves, diag_blocks, panel_blocks, ancestors, target_ids, target_tiles):
    me, half = lax.axis_index("col"), lax.axis_index("row")
    paired = halves == 2 and panel_blocks.shape[0] == 2
    swap = [(0, 1), (1, 0)]
    if paired:
        outgoing = lax.dynamic_index_in_dim(panel_blocks, 1 - half, 0, keepdims=False).astype(BF16)
        other = lax.ppermute(outgoing, "row", swap)
    spread = lax.optimization_barrier(jnp.broadcast_to(target_ids, (8, 128)))
    all_ids = lax.optimization_barrier(lax.all_gather(spread, "col", axis=0, tiled=True))
    all_ids = all_ids.reshape(columns, 8, 128)[:, 0, 0]
    matches = ancestors[:, :, None] == all_ids[None, None, :]
    place = jnp.arange(columns, dtype=jnp.int32)
    position = jnp.sum(jnp.where(matches, place[None, None, :], 0), axis=2)
    distance = (position ^ me).astype(jnp.int32)
    bits = list(range(columns.bit_length() - 1))
    slot = jnp.zeros_like(distance)
    for bit in bits:
        slot = slot * 2 + ((distance >> bit) & 1)
    hi, lo = inverse_factors(diag_blocks)
    if not paired:
        panel_factor, tiles = gathered(slot, panel_blocks, hi, lo, columns)
        rows = tiles.shape[1]
        keep, send = tiles[: columns // 2], tiles[columns // 2 :].astype(BF16)
        return (panel_factor, target_tiles - halve_and_add(keep, send, bits, columns, rows)[None])
    mine = half.astype(jnp.int32).reshape(1)
    panel_factor, same_keep, same_send, cross_keep, cross_send = panel_products(
        slot, mine, panel_blocks, other, hi, lo, columns
    )
    rows = panel_blocks.shape[2]
    same = halve_and_add(same_keep, same_send, bits, columns, rows)
    diagonal = same[rows : rows + 1] + same[rows + 1 : rows + 2]
    same = same[:rows] + jnp.where(jnp.eye(rows, dtype=bool), diagonal, 0.0)
    cross = halve_and_add(cross_keep, cross_send, bits, columns, rows)
    back = lax.ppermute(cross.astype(BF16), "row", swap)
    cross = cross + back.astype(F32).T
    update = jnp.where(
        half == 0,
        jnp.concatenate([same, cross], axis=1),
        jnp.concatenate([cross, same], axis=1),
    )
    return (panel_factor, target_tiles - update[None])


def solution(mesh):
    in_specs = (
        P("col", None, None),
        P("col", None, "row", None),
        P("col", None),
        P("col"),
        P("col", "row", None),
    )
    out_specs = (P("col", None, "row", None), P("col", "row", None))
    return jax.shard_map(
        functools.partial(on_device, mesh.shape["col"], mesh.shape["row"]),
        mesh=mesh,
        in_specs=in_specs,
        out_specs=out_specs,
        check_vma=False,
    )
```

time: 574 us -> 135 us (0.24); the launches traced: 565 us -> 135 us
  other arithmetic: 249 us -> 4.42 us
  waiting for transfers between devices: 196 us -> 42.5 us
  Pallas kernels: 0 us -> 51.1 us
  matrix products: 44.8 us -> 0 us
  local copies, waits for them, and re-layouts: 46.1 us -> 6.53 us
  between operations: 15.4 us -> 1.61 us
  blocking collectives: 13.7 us -> 21.8 us
  starting transfers between devices: 0.08 us -> 6.78 us
    another operation x20 -> x0, other arithmetic: 235 us -> none  [the longest x16 154 us: solve_local(): factor = jnp.linalg.cholesky(diag_block)]
    reduce_scatter x1 -> x0, waiting for transfers between devices: 105 us -> none  [on_device(): update = lax.psum_scatter(term, 'col', scatter_dimension=0, tiled=True)]
    all_gather x1 -> x0, waiting for transfers between devices: 90.8 us -> none  [on_device(): lax.all_gather(rounded, 'row', axis=2, tiled=True)]
    pallas_call x0 -> x2, Pallas kernels: none -> 51.1 us  [the longest x1 29.1 us: inverse_factors(): pl.pallas_call(factor_kernel, out_shape=(out, out), in_specs=[pl.BlockSpe...]
    ppermute x0 -> x10, waiting for transfers between devices: none -> 42.5 us  [the longest x8 42.5 us: halve_and_add(): got = lax.ppermute(send, 'col', [(c, c ^ 1 << bit) for c in range(columns)])]
    another operation x13 -> x0, matrix products: 28.4 us -> none  [the longest x7 21.7 us: solve_local(): solved = jax.scipy.linalg.solve_triangular(factor, rhs, lower=True)]
    all_gather x0 -> x1, blocking collectives: none -> 21.8 us  [on_device(): lax.all_gather(spread, 'col', axis=0, tiled=True)]
    dot_general x2 -> x0, matrix products: 16.3 us -> none  [the longest x1 9.28 us: spread_terms(): jnp.einsum('cn,cab->nab', onehot, flat_products, precision=lax.Precision....]
  transfers between devices with their start and end apart: 2 -> 10, of which waited for: 2 -> 5; matrix products, arithmetic and copies ran while one was open for 0% -> 3% of each run, Pallas kernels for 0% -> 22%
where the time goes in v1:
time: 135 us
  Pallas kernels  51.1 us (38%)
  waiting for transfers between devices  42.5 us (31%)
  blocking collectives  21.8 us (16%)
  starting transfers between devices  6.78 us (5%)
  local copies, waits for them, and re-layouts  6.53 us (5%)
  other arithmetic  4.42 us (3%)
  between operations  1.61 us (1%)
    ppermute x8, waiting for transfers between devices, halve_and_add(): got = lax.ppermute(send, 'col', [(c, c ^ 1 << bit) for c in range(columns)])  42.5 us
    pallas_call x1, Pallas kernels, inverse_factors(): pl.pallas_call(factor_kernel, out_shape=(out, out), in_specs=[pl.BlockSpe...  29.1 us
    pallas_call x1, Pallas kernels, panel_products(): pl.pallas_call(panel_kernel, out_shape=[jax.ShapeDtypeStruct(panel_blocks...  22 us
    all_gather x1, blocking collectives, on_device(): lax.all_gather(spread, 'col', axis=0, tiled=True)  21.8 us
    convert_element_type x1, local copies, waits for them, and re-layouts, on_device(): lax.dynamic_index_in_dim(panel_blocks, 1 - half, 0, keepdims=False)  3.93 us
    ppermute x1, starting transfers between devices, on_device(): other = lax.ppermute(outgoing, 'row', swap)  2.94 us
    ppermute x8, starting transfers between devices, halve_and_add(): got = lax.ppermute(send, 'col', [(c, c ^ 1 << bit) for c in range(columns)])  2.93 us
  transfers between devices with their start and end apart: 10, of which 5 were waited for; matrix products, arithmetic and copies ran while one was open for 3% of the time, Pallas kernels for 22%

profile of v1, /device:TPU:0, one launch (start us, length us, event | category | flops | bytes accessed | tf_op | source)
XLA Modules:
  0.0 134.7 jit_solution(10280451410295976270)
XLA Ops:
  0.6 0.0 copy-start.5
  0.6 0.0 copy-start.2
  0.7 3.9 %fusion = bf16[8,256,512]{2,1,0:T(8,128)(2,1)} fusion(f32[2,8,256,512]{3,2,1,0:T(8,128)} %panel_ref.1, s32[]{:T(128)S(6)} %select_n.54), kind=kLoop, calls=%fused_computation.2 | loop fusion | bytes 4194308 | tf_op jit(solution)/shard_map/convert_element_type | solution.py:254
  4.6 2.9 %collective-permute-start = (bf16[8,256,512]{2,1,0:T(8,128)(2,1)}, bf16[8,256,512]{2,1,0:T(8,128)(2,1)}, u32[]{:S(2)}, u32[]{:S(2)}) collective-permute-start(bf16[8,256,512]{2,1,0:T(8,128)(2,1)} %fusion), channel_id=1, source_target_pairs={{0,1},{1,0},{2,3},{3,2},{4,5},{5,4},{6,7},{7,6},{8,9},{9,8},{10,11... | collective-permute-start | bytes 6291464 | tf_op jit(solution)/shard_map/ppermute | solution.py:255
  8.2 21.8 %all_gather.3 = s32[128,128]{1,0:T(8,128)S(1)} all-gather(s32[8,128]{1,0:T(8,128)S(1)} %broadcast_in_dim.83), channel_id=1, replica_groups=mesh['col'=16,'row'=2] {'col'}, dimensions={0}, use_global_device_ids=true | all-gather | bytes 69632 | tf_op jit(solution)/shard_map/all_gather | solution.py:257
  30.0 0.4 slice_reduce_fusion
  30.4 0.0 copy-done.5
  30.4 0.2 select_reduce_fusion
  30.6 0.6 and_add_fusion.slot_ref
  31.2 0.0 copy-done.2
  31.2 29.1 %factor.1 = (bf16[2,512,512]{2,1,0:T(8,128)(2,1)S(1)}, bf16[2,512,512]{2,1,0:T(8,128)(2,1)S(1)}) custom-call(f32[2,512,512]{2,1,0:T(8,128)S(1)} %copy-done.2), custom_call_target="tpu_custom_call" | custom-call | flops 40000000000 | bytes 2097152 | tf_op jit(solution)/shard_map/factor/pallas_call | solution.py:100
  60.3 0.0 copy-start
  60.3 1.0 copy-done
  61.3 1.0 copy-done.1
  62.3 0.0 collective-permute-done.other_ref
  62.3 22.0 %panel.1 = (f32[2,8,256,512]{3,2,1,0:T(8,128)}, bf16[8,272,256]{2,1,0:T(8,128)(2,1)}, bf16[8,272,256]{2,1,0:T(8,128)(2,1)}, bf16[8,256,256]{2,1,0:T(8,128)(2,1)}, bf16[8,256,256]{2,1,0:T(8,128)(2,1)}) custom-call(s32[2,8]{1,0:T(2,128)} %and_add_fusion.slot_ref, s32[1]{0:T(128)} %bitcast.2.mine_ref, f32[2,8,256,512]{3,2,1,0:T(8,128)} %panel_ref.1, ...), custom_call_target="tpu_custom_call" | custom-call | tf_op jit(solution)/shard_map/panel/pallas_call | solution.py:198
  84.3 0.3 collective-permute-start.5
  84.6 0.2 collective-permute-start.1
  84.8 2.4 %collective-permute-done.5 = bf16[8,256,256]{2,1,0:T(8,128)(2,1)S(1)} collective-permute-done((bf16[8,256,256]{2,1,0:T(8,128)(2,1)}, bf16[8,256,256]{2,1,0:T(8,128)(2,1)S(1)}, u32[]{:S(2)}, u32[]{:S(2)}) %collective-permute-start.5) | collective-permute-done | bytes 1048608 | tf_op jit(solution)/shard_map/ppermute | solution.py:228
  87.2 1.5 %convert_add_fusion.1 = f32[8,256,256]{2,1,0:T(8,128)S(1)} fusion(bf16[8,256,256]{2,1,0:T(8,128)(2,1)S(1)} %collective-permute-done.5, bf16[8,256,256]{2,1,0:T(8,128)(2,1)} %get-tuple-element.14), kind=kLoop, calls=%fused_computation.3 | loop fusion | flops 1572864 | bytes 4194304 | tf_op jit(solution)/shard_map/add | solution.py:229
  88.7 0.1 slice.182
  88.8 0.1 collective-permute-start.6
  88.8 0.0 collective-permute-done.1
  88.8 0.0 copy-done.3
  88.9 0.2 convert_add_fusion
  89.1 0.2 fusion.2
  89.3 2.1 %collective-permute-start.2 = (bf16[4,272,256]{2,1,0:T(8,128)(2,1)S(1)}, bf16[4,272,256]{2,1,0:T(8,128)(2,1)S(1)}, u32[]{:S(2)}, u32[]{:S(2)}) collective-permute-start(bf16[4,272,256]{2,1,0:T(8,128)(2,1)S(1)} %fusion.2), channel_id=1, source_target_pairs={{0,4},{2,6},{4,0},{6,2},{8,12},{10,14},{12,8},{14,10},{16,20},{18,... | collective-permute-start | bytes 1671176 | tf_op jit(solution)/shard_map/ppermute | solution.py:228
  91.4 12.2 %collective-permute-done.6 = bf16[4,256,256]{2,1,0:T(8,128)(2,1)S(1)} collective-permute-done((bf16[4,256,256]{2,1,0:T(8,128)(2,1)S(1)}, bf16[4,256,256]{2,1,0:T(8,128)(2,1)S(1)}, u32[]{:S(2)}, u32[]{:S(2)}) %collective-permute-start.6) | collective-permute-done | bytes 524320 | tf_op jit(solution)/shard_map/ppermute | solution.py:228
  103.6 0.1 slice_add_fusion.1
  103.7 0.1 collective-permute-start.7
  103.8 11.1 %collective-permute-done.2 = bf16[4,272,256]{2,1,0:T(8,128)(2,1)S(1)} collective-permute-done((bf16[4,272,256]{2,1,0:T(8,128)(2,1)S(1)}, bf16[4,272,256]{2,1,0:T(8,128)(2,1)S(1)}, u32[]{:S(2)}, u32[]{:S(2)}) %collective-permute-start.2) | collective-permute-done | bytes 557088 | tf_op jit(solution)/shard_map/ppermute | solution.py:228
  114.9 0.1 slice_add_fusion
  115.1 0.1 fusion.4
  115.2 0.1 collective-permute-start.3
  115.3 0.0 collective-permute-done.7
  115.3 0.1 slice_add_fusion.3
  115.4 0.0 copy-start.4
  115.4 0.1 collective-permute-start.8
  115.5 10.7 %collective-permute-done.3 = bf16[2,272,256]{2,1,0:T(8,128)(2,1)S(1)} collective-permute-done((bf16[2,272,256]{2,1,0:T(8,128)(2,1)S(1)}, bf16[2,272,256]{2,1,0:T(8,128)(2,1)S(1)}, u32[]{:S(2)}, u32[]{:S(2)}) %collective-permute-start.3) | collective-permute-done | bytes 278560 | tf_op jit(solution)/shard_map/ppermute | solution.py:228
  126.2 0.1 slice_add_fusion.2
  126.3 0.1 fusion.7
  126.4 0.1 collective-permute-start.4
  126.5 0.0 collective-permute-done.8
  126.5 0.1 copy.10
  126.7 0.9 collective-permute-start.9
  127.6 6.1 %collective-permute-done.4 = bf16[1,272,256]{2,1,0:T(8,128)(2,1)S(1)} collective-permute-done((bf16[1,272,256]{2,1,0:T(8,128)(2,1)S(1)}, bf16[1,272,256]{2,1,0:T(8,128)(2,1)S(1)}, u32[]{:S(2)}, u32[]{:S(2)}) %collective-permute-start.4) | collective-permute-done | bytes 139296 | tf_op jit(solution)/shard_map/ppermute | solution.py:228
  133.7 0.0 collective-permute-done.9
  133.8 0.9 fusion.5
  (18 shorter events, 0.2 us)
Async XLA Ops:
  0.6 29.7 %copy-start.5 = (s32[2,8]{1,0:T(2,128)S(1)}, s32[2,8]{1,0:T(2,128)}, u32[]{:S(2)}) copy-start(s32[2,8]{1,0:T(2,128)} %param.7) | copy-start | bytes 196
  0.6 30.5 %copy-start.2 = (f32[2,512,512]{2,1,0:T(8,128)S(1)}, f32[2,512,512]{2,1,0:T(8,128)}, u32[]{:S(2)}) copy-start(f32[2,512,512]{2,1,0:T(8,128)} %diag_ref.1) | copy-start | bytes 6291460
  4.6 57.7 %collective-permute-start = (bf16[8,256,512]{2,1,0:T(8,128)(2,1)}, bf16[8,256,512]{2,1,0:T(8,128)(2,1)}, u32[]{:S(2)}, u32[]{:S(2)}) collective-permute-start(bf16[8,256,512]{2,1,0:T(8,128)(2,1)} %fusion), channel_id=1, source_target_pairs={{0,1},{1,0},{2,3},{3,2},{4,5},{5,4},{6,7},{7,6},{8,9},{9,8},{10,11... | collective-permute-start | bytes 6291464 | tf_op jit(solution)/shard_map/ppermute | solution.py:255
  60.3 1.0 copy-start
  61.3 1.0 copy-start.1
  84.3 2.9 %collective-permute-start.5 = (bf16[8,256,256]{2,1,0:T(8,128)(2,1)}, bf16[8,256,256]{2,1,0:T(8,128)(2,1)S(1)}, u32[]{:S(2)}, u32[]{:S(2)}) collective-permute-start(bf16[8,256,256]{2,1,0:T(8,128)(2,1)} %get-tuple-element.15), channel_id=1, source_target_pairs={{0,2},{2,0},{4,6},{6,4},{8,10},{10,8},{12,14},{14,12},{16,18},{18,... | collective-permute-start | bytes 3145736 | tf_op jit(solution)/shard_map/ppermute | solution.py:228
  84.6 4.2 %collective-permute-start.1 = (bf16[8,272,256]{2,1,0:T(8,128)(2,1)}, bf16[8,272,256]{2,1,0:T(8,128)(2,1)S(1)}, u32[]{:S(2)}, u32[]{:S(2)}) collective-permute-start(bf16[8,272,256]{2,1,0:T(8,128)(2,1)} %get-tuple-element.13), channel_id=1, source_target_pairs={{0,2},{2,0},{4,6},{6,4},{8,10},{10,8},{12,14},{14,12},{16,18},{18,... | collective-permute-start | bytes 3342344 | tf_op jit(solution)/shard_map/ppermute | solution.py:228
  87.1 1.7 %copy-start.3 = (bf16[8,272,256]{2,1,0:T(8,128)(2,1)S(1)}, bf16[8,272,256]{2,1,0:T(8,128)(2,1)}, u32[]{:S(2)}) copy-start(bf16[8,272,256]{2,1,0:T(8,128)(2,1)} %get-tuple-element.12) | copy-start | bytes 3342340
  88.8 14.8 %collective-permute-start.6 = (bf16[4,256,256]{2,1,0:T(8,128)(2,1)S(1)}, bf16[4,256,256]{2,1,0:T(8,128)(2,1)S(1)}, u32[]{:S(2)}, u32[]{:S(2)}) collective-permute-start(bf16[4,256,256]{2,1,0:T(8,128)(2,1)S(1)} %slice.182), channel_id=1, source_target_pairs={{0,4},{2,6},{4,0},{6,2},{8,12},{10,14},{12,8},{14,10},{16,20},{18,... | collective-permute-start | bytes 1572872 | tf_op jit(solution)/shard_map/ppermute | solution.py:228
  89.3 25.6 %collective-permute-start.2 = (bf16[4,272,256]{2,1,0:T(8,128)(2,1)S(1)}, bf16[4,272,256]{2,1,0:T(8,128)(2,1)S(1)}, u32[]{:S(2)}, u32[]{:S(2)}) collective-permute-start(bf16[4,272,256]{2,1,0:T(8,128)(2,1)S(1)} %fusion.2), channel_id=1, source_target_pairs={{0,4},{2,6},{4,0},{6,2},{8,12},{10,14},{12,8},{14,10},{16,20},{18,... | collective-permute-start | bytes 1671176 | tf_op jit(solution)/shard_map/ppermute | solution.py:228
  103.7 11.6 %collective-permute-start.7 = (bf16[2,256,256]{2,1,0:T(8,128)(2,1)S(1)}, bf16[2,256,256]{2,1,0:T(8,128)(2,1)S(1)}, u32[]{:S(2)}, u32[]{:S(2)}) collective-permute-start(bf16[2,256,256]{2,1,0:T(8,128)(2,1)S(1)} %slice.183), channel_id=1, source_target_pairs={{0,8},{2,10},{4,12},{6,14},{8,0},{10,2},{12,4},{14,6},{16,24},{18,... | collective-permute-start | bytes 786440 | tf_op jit(solution)/shard_map/ppermute | solution.py:228
  115.2 11.0 %collective-permute-start.3 = (bf16[2,272,256]{2,1,0:T(8,128)(2,1)S(1)}, bf16[2,272,256]{2,1,0:T(8,128)(2,1)S(1)}, u32[]{:S(2)}, u32[]{:S(2)}) collective-permute-start(bf16[2,272,256]{2,1,0:T(8,128)(2,1)S(1)} %fusion.4), channel_id=1, source_target_pairs={{0,8},{2,10},{4,12},{6,14},{8,0},{10,2},{12,4},{14,6},{16,24},{18,... | collective-permute-start | bytes 835592 | tf_op jit(solution)/shard_map/ppermute | solution.py:228
  115.4 18.4 %copy-start.4 = (f32[1,256,512]{2,1,0:T(8,128)S(1)}, f32[1,256,512]{2,1,0:T(8,128)}, u32[]{:S(2)}) copy-start(f32[1,256,512]{2,1,0:T(8,128)} %param.9) | copy-start | bytes 1572868
  115.4 11.1 %collective-permute-start.8 = (bf16[1,256,256]{2,1,0:T(8,128)(2,1)S(1)}, bf16[1,256,256]{2,1,0:T(8,128)(2,1)S(1)}, u32[]{:S(2)}, u32[]{:S(2)}) collective-permute-start(bf16[1,256,256]{2,1,0:T(8,128)(2,1)S(1)} %slice.184), channel_id=1, source_target_pairs={{0,16},{2,18},{4,20},{6,22},{8,24},{10,26},{12,28},{14,30},{16,0},... | collective-permute-start | bytes 393224 | tf_op jit(solution)/shard_map/ppermute | solution.py:228
  126.4 7.2 %collective-permute-start.4 = (bf16[1,272,256]{2,1,0:T(8,128)(2,1)S(1)}, bf16[1,272,256]{2,1,0:T(8,128)(2,1)S(1)}, u32[]{:S(2)}, u32[]{:S(2)}) collective-permute-start(bf16[1,272,256]{2,1,0:T(8,128)(2,1)S(1)} %fusion.7), channel_id=1, source_target_pairs={{0,16},{2,18},{4,20},{6,22},{8,24},{10,26},{12,28},{14,30},{16,0},... | collective-permute-start | bytes 417800 | tf_op jit(solution)/shard_map/ppermute | solution.py:228
  126.7 7.1 %collective-permute-start.9 = (bf16[256,256]{0,1:T(8,128)(2,1)S(1)}, bf16[256,256]{0,1:T(8,128)(2,1)S(1)}, u32[]{:S(2)}, u32[]{:S(2)}) collective-permute-start(bf16[256,256]{0,1:T(8,128)(2,1)S(1)} %copy.10), channel_id=1, source_target_pairs={{0,1},{1,0},{2,3},{3,2},{4,5},{5,4},{6,7},{7,6},{8,9},{9,8},{10,11... | collective-permute-start | bytes 393224 | tf_op jit(solution)/shard_map/ppermute | solution.py:282

commit v2 on v1

--- a/solution.py
+++ b/solution.py
@@ -118,6 +118,15 @@
     return lax.dot_general(a, b, (((1,), (1,)), ((), ())), preferred_element_type=F32)
 
 
+def split_diagonal(tail, first, second, extra):
+    rest = 0.0
+    for at, term in ((0, first), (2, second)):
+        total = tail[at : at + 1] + tail[at + 1 : at + 2] + term
+        top = total.astype(BF16).astype(F32)
+        rest = jnp.where(extra == at, top, jnp.where(extra == at + 1, total - top, rest))
+    return rest
+
+
 def place_tile(tile, slot, keep_ref, send_ref):
     half = keep_ref.shape[0]
 
@@ -158,18 +167,18 @@
     diagonal = lax.broadcasted_iota(jnp.int32, (rows, rows), 0) == lax.broadcasted_iota(
         jnp.int32, (rows, rows), 1
     )
-    extra = lax.broadcasted_iota(jnp.int32, (16, rows), 0)
+    extra = lax.broadcasted_iota(jnp.int32, (16, NB), 0)
     for i in range(blocks):
         product = dot_nt(rounded[i], rounded[i])
         sums = jnp.sum(jnp.where(diagonal, product, 0.0), axis=0, keepdims=True)
         product = jnp.where(diagonal, 0.0, product)
+        lower = [product[:NB, :NB], product[NB:, :NB], product[NB:, NB:]]
 
         def added(old):
-            tail = old[rows:].astype(F32)
-            total = jnp.sum(tail, axis=0, keepdims=True) + sums
-            top = total.astype(BF16).astype(F32)
-            rest = jnp.where(extra == 0, top, jnp.where(extra == 1, total - top, 0.0))
-            return jnp.concatenate([old[:rows].astype(F32) + product, rest], axis=0).astype(BF16)
+            rest = split_diagonal(old[3 * NB :].astype(F32), sums[:, :NB], sums[:, NB:], extra)
+            return jnp.concatenate(
+                [old[: 3 * NB].astype(F32) + jnp.concatenate(lower, axis=0), rest], axis=0
+            ).astype(BF16)
 
         place_tile(added, slot_ref[s, j * blocks + i], same_keep, same_send)
 
@@ -179,15 +188,25 @@
         partner = (times_inverse(got, hi) + times_inverse(got, lo)).astype(BF16)
         partner = partner.reshape(blocks, rows, width)
         for i in range(blocks):
-            product = dot_nt(rounded[i], partner[i]).astype(BF16)
-            place_tile(lambda old: product, slot_ref[s, j * blocks + i], cross_keep, cross_send)
+            slot = slot_ref[s, j * blocks + i]
+            first, second = rounded[i], partner[i]
+
+            @pl.when(mine_ref[0] == 0)
+            def _():
+                product = dot_nt(first, second).astype(BF16)
+                place_tile(lambda old: product, slot, cross_keep, cross_send)
+
+            @pl.when(mine_ref[0] != 0)
+            def _():
+                product = dot_nt(second, first).astype(BF16)
+                place_tile(lambda old: product, slot, cross_keep, cross_send)
 
 
 def panel_products(slot, mine, panel_blocks, other, hi, lo, targets):
     count, blocks, rows, width = panel_blocks.shape
     step = 2 if blocks % 2 == 0 else 1
     steps = blocks // step
-    shapes = [(targets // 2, rows + 16, rows)] * 2 + [(targets // 2, rows, rows)] * 2
+    shapes = [(targets // 2, 3 * NB + 16, NB)] * 2 + [(targets // 2, rows, rows)] * 2
     whole = [pl.BlockSpec(shape, lambda s, j, slot, mine: (0, 0, 0)) for shape in shapes]
     factor = pl.BlockSpec((1, width, width), lambda s, j, slot, mine: (s, 0, 0))
     panel = pl.BlockSpec((1, step, rows, width), lambda s, j, slot, mine: (s, j, 0, 0))
@@ -212,25 +231,266 @@
     )(slot, mine, panel_blocks, other, hi, lo)
 
 
-def packed(value, rows):
-    if value.shape[-2] == rows:
-        return value.astype(BF16)
-    total = value[..., rows : rows + 1, :] + value[..., rows + 1 : rows + 2, :]
-    top = lax.reduce_precision(total, 8, 7)
-    row = lax.broadcasted_iota(jnp.int32, value.shape, value.ndim - 2)
-    value = jnp.where(row == rows, top, jnp.where(row == rows + 1, total - top, value))
-    return value.astype(BF16)
-
-
-def halve_and_add(keep, send, order, columns, rows):
+def halve_and_add(keep, send, order, columns):
     shape = keep.shape[1:]
-    for step, bit in enumerate(order):
+    for bit in order:
         got = lax.ppermute(send, "col", [(c, c ^ (1 << bit)) for c in range(columns)])
         value = keep.astype(F32) + got.astype(F32)
         half = value.shape[0] // 2
         if half:
-            keep, send = value[:half], packed(value[half:], rows)
+            keep, send = value[:half], value[half:].astype(BF16)
     return value.reshape(shape)
+
+
+def flipped(index, bits):
+    bit = 1
+    other = index
+    while bit <= bits:
+        if bits & bit:
+            other = other + bit * (1 - 2 * ((index // bit) % 2))
+        bit *= 2
+    return other
+
+
+def meet(peers):
+    barrier = pltpu.get_barrier_semaphore()
+    for peer in peers:
+        pl.semaphore_signal(barrier, inc=1, device_id=peer, device_id_type=pl.DeviceIdType.MESH)
+    pl.semaphore_wait(barrier, len(peers))
+
+
+def ids_kernel(own_ref, out_ref, landed, send_sem, recv_sem):
+    columns = out_ref.shape[0]
+    me, half = lax.axis_index("col"), lax.axis_index("row")
+    peers = [(flipped(me, q), half) for q in range(1, columns)]
+    meet(peers)
+    copies = []
+    for q in range(1, columns):
+        copy = pltpu.make_async_remote_copy(
+            src_ref=own_ref,
+            dst_ref=landed.at[q],
+            send_sem=send_sem.at[q],
+            recv_sem=recv_sem.at[q],
+            device_id=peers[q - 1],
+            device_id_type=pl.DeviceIdType.MESH,
+        )
+        copy.start()
+        copies.append(copy)
+    out_ref[0] = own_ref[...]
+    for q, copy in enumerate(copies, 1):
+        copy.wait()
+        out_ref[q] = landed[q]
+
+
+def ids_by_distance(target_ids, columns):
+    own = jnp.broadcast_to(target_ids, (8, 128))
+    out = pl.pallas_call(
+        ids_kernel,
+        out_shape=jax.ShapeDtypeStruct((columns, 8, 128), jnp.int32),
+        in_specs=[pl.BlockSpec(memory_space=pltpu.VMEM)],
+        out_specs=pl.BlockSpec(memory_space=pltpu.VMEM),
+        scratch_shapes=[
+            pltpu.VMEM((columns, 8, 128), jnp.int32),
+            pltpu.SemaphoreType.DMA((columns,)),
+            pltpu.SemaphoreType.DMA((columns,)),
+        ],
+        compiler_params=pltpu.CompilerParams(collective_id=0, has_side_effects=True),
+        name="ids",
+    )(own)
+    return out[:, 0, 0]
+
+
+def reduce_kernel(
+    order, same_keep, same_send, cross_keep, cross_send, target_ref, out_ref,
+    same_acc, same_out, same_got, cross_acc, cross_out, cross_got0, cross_got,
+    swap_out, swap_got, last_out, last_got, full, send_sem, recv_sem,
+):
+    me, half = lax.axis_index("col"), lax.axis_index("row")
+    partner = (me, 1 - half)
+    peers = [(flipped(me, 1 << bit), half) for bit in order]
+    stages = len(order)
+    rows = 2 * NB
+    meet(peers + [partner])
+    extra = lax.broadcasted_iota(jnp.int32, (16, NB), 0)
+    kept_rows = pl.ds(pl.multiple_of(half * NB, NB), NB)
+    sent_rows = pl.ds(pl.multiple_of((1 - half) * NB, NB), NB)
+    count = same_keep.shape[0]
+    sizes = [count >> t for t in range(stages)]
+    starts = [sum(sizes[1:t]) for t in range(stages)]
+
+    def remote(number, src, dst, device):
+        copy = pltpu.make_async_remote_copy(
+            src_ref=src,
+            dst_ref=dst,
+            send_sem=send_sem.at[number],
+            recv_sem=recv_sem.at[number],
+            device_id=device,
+            device_id_type=pl.DeviceIdType.MESH,
+        )
+        copy.start()
+        return copy
+
+    def same_stage(t):
+        size = sizes[t]
+        base = 0 if t == 0 else count + starts[t]
+
+        def total(q):
+            mine = same_keep[q].astype(F32) if t == 0 else same_acc[q]
+            return mine + same_got[base + q].astype(F32)
+
+        if size == 1:
+            same_acc[0] = total(0)
+            return None
+        send_at = starts[t + 1]
+
+        def send_tile(i, carry):
+            value = total(size // 2 + i)
+            rest = split_diagonal(value[3 * NB :], 0.0, 0.0, extra)
+            same_out[send_at + i] = jnp.concatenate([value[: 3 * NB], rest], axis=0).astype(BF16)
+            return carry
+
+        lax.fori_loop(0, size // 2, send_tile, 0)
+        copy = remote(
+            t + 1,
+            same_out.at[pl.ds(send_at, size // 2)],
+            same_got.at[pl.ds(count + send_at, size // 2)],
+            peers[t + 1],
+        )
+
+        def keep_tile(q, carry):
+            same_acc[q] = total(q)
+            return carry
+
+        lax.fori_loop(0, size // 2, keep_tile, 0)
+        return copy
+
+    def cross_first():
+        def send_tile(q, carry):
+            value = cross_keep[q, sent_rows, :].astype(F32) + cross_got0[q, sent_rows, :].astype(F32)
+            swap_out[q] = value.astype(BF16)
+            return carry
+
+        lax.fori_loop(0, count, send_tile, 0)
+        copy = remote(2 * stages, swap_out, swap_got, partner)
+
+        def keep_tile(q, carry):
+            cross_acc[q] = cross_keep[q, kept_rows, :].astype(F32) + cross_got0[
+                q, kept_rows, :
+            ].astype(F32)
+            return carry
+
+        lax.fori_loop(0, count, keep_tile, 0)
+        return copy
+
+    def cross_stage(t):
+        size = sizes[t]
+
+        def total(q):
+            other = swap_got[q] if t == 0 else cross_got[starts[t] + q]
+            return cross_acc[q] + other.astype(F32)
+
+        if size == 1:
+            cross_acc[0] = total(0)
+            return None
+        send_at = starts[t + 1]
+
+        def send_tile(i, carry):
+            cross_out[send_at + i] = total(size // 2 + i).astype(BF16)
+            return carry
+
+        lax.fori_loop(0, size // 2, send_tile, 0)
+        copy = remote(
+            stages + t + 1,
+            cross_out.at[pl.ds(send_at, size // 2)],
+            cross_got.at[pl.ds(send_at, size // 2)],
+            peers[t + 1],
+        )
+
+        def keep_tile(q, carry):
+            cross_acc[q] = total(q)
+            return carry
+
+        lax.fori_loop(0, size // 2, keep_tile, 0)
+        return copy
+
+    cross_copy = remote(stages, cross_send, cross_got0, peers[0])
+    same_copy = remote(0, same_send, same_got.at[pl.ds(0, count)], peers[0])
+    cross_copy.wait()
+    swap_copy = cross_first()
+    same_copy.wait()
+    same_copy = same_stage(0)
+    cross_copy = swap_copy
+    for t in range(stages):
+        if t + 1 < stages:
+            same_copy.wait()
+            same_copy = same_stage(t + 1)
+        cross_copy.wait()
+        cross_copy = cross_stage(t)
+    last_out[...] = cross_acc[0].astype(BF16)
+    copy = remote(2 * stages + 1, last_out, last_got, partner)
+
+    value = same_acc[0]
+    d = value[3 * NB :]
+    below = value[NB : 2 * NB]
+    diagonal = jnp.concatenate([d[0:1] + d[1:2], d[2:3] + d[3:4]], axis=1)
+    same = jnp.concatenate(
+        [
+            jnp.concatenate([value[:NB], below.T], axis=1),
+            jnp.concatenate([below, value[2 * NB : 3 * NB]], axis=1),
+        ],
+        axis=0,
+    )
+    eye = lax.broadcasted_iota(jnp.int32, (rows, rows), 0) == lax.broadcasted_iota(
+        jnp.int32, (rows, rows), 1
+    )
+    same = jnp.where(eye, diagonal, same)
+    full[kept_rows, :] = cross_acc[0]
+    copy.wait()
+    full[sent_rows, :] = last_got[...].astype(F32)
+
+    @pl.when(half == 0)
+    def _():
+        out_ref[0, :, :rows] = target_ref[0, :, :rows] - same
+        out_ref[0, :, rows:] = target_ref[0, :, rows:] - full[...]
+
+    @pl.when(half == 1)
+    def _():
+        out_ref[0, :, :rows] = target_ref[0, :, :rows] - full[...].T
+        out_ref[0, :, rows:] = target_ref[0, :, rows:] - same
+
+
+def reduced(order, same_keep, same_send, cross_keep, cross_send, target_tiles):
+    count, rows = cross_keep.shape[:2]
+    tile = same_keep.shape[1:]
+    part = (NB, rows)
+    stages = len(order)
+    vmem = pl.BlockSpec(memory_space=pltpu.VMEM)
+    return pl.pallas_call(
+        functools.partial(reduce_kernel, order),
+        out_shape=jax.ShapeDtypeStruct(target_tiles.shape, F32),
+        in_specs=[vmem] * 5,
+        out_specs=vmem,
+        scratch_shapes=[
+            pltpu.VMEM((count,) + tile, F32),
+            pltpu.VMEM((count,) + tile, BF16),
+            pltpu.VMEM((2 * count,) + tile, BF16),
+            pltpu.VMEM((count,) + part, F32),
+            pltpu.VMEM((count,) + part, BF16),
+            pltpu.VMEM((count, rows, rows), BF16),
+            pltpu.VMEM((count,) + part, BF16),
+            pltpu.VMEM((count,) + part, BF16),
+            pltpu.VMEM((count,) + part, BF16),
+            pltpu.VMEM(part, BF16),
+            pltpu.VMEM(part, BF16),
+            pltpu.VMEM((rows, rows), F32),
+            pltpu.SemaphoreType.DMA((2 * stages + 2,)),
+            pltpu.SemaphoreType.DMA((2 * stages + 2,)),
+        ],
+        compiler_params=pltpu.CompilerParams(
+            collective_id=1, has_side_effects=True, vmem_limit_bytes=48 * 2**20
+        ),
+        name="reduce",
+    )(same_keep, same_send, cross_keep, cross_send, target_tiles)
 
 
 def gathered(slot, panel_blocks, hi, lo, columns):
@@ -248,18 +508,21 @@
 
 def on_device(columns, halves, diag_blocks, panel_blocks, ancestors, target_ids, target_tiles):
     me, half = lax.axis_index("col"), lax.axis_index("row")
-    paired = halves == 2 and panel_blocks.shape[0] == 2
+    paired = halves == 2 and panel_blocks.shape[0] == 2 and panel_blocks.shape[2] == 2 * NB
     swap = [(0, 1), (1, 0)]
     if paired:
         outgoing = lax.dynamic_index_in_dim(panel_blocks, 1 - half, 0, keepdims=False).astype(BF16)
         other = lax.ppermute(outgoing, "row", swap)
-    spread = lax.optimization_barrier(jnp.broadcast_to(target_ids, (8, 128)))
-    all_ids = lax.optimization_barrier(lax.all_gather(spread, "col", axis=0, tiled=True))
-    all_ids = all_ids.reshape(columns, 8, 128)[:, 0, 0]
-    matches = ancestors[:, :, None] == all_ids[None, None, :]
     place = jnp.arange(columns, dtype=jnp.int32)
-    position = jnp.sum(jnp.where(matches, place[None, None, :], 0), axis=2)
-    distance = (position ^ me).astype(jnp.int32)
+    if paired:
+        near_ids = ids_by_distance(target_ids, columns)
+        matches = ancestors[:, :, None] == near_ids[None, None, :]
+        distance = jnp.sum(jnp.where(matches, place[None, None, :], 0), axis=2)
+    else:
+        all_ids = lax.all_gather(target_ids, "col", axis=0, tiled=True)
+        matches = ancestors[:, :, None] == all_ids[None, None, :]
+        position = jnp.sum(jnp.where(matches, place[None, None, :], 0), axis=2)
+        distance = (position ^ me).astype(jnp.int32)
     bits = list(range(columns.bit_length() - 1))
     slot = jnp.zeros_like(distance)
     for bit in bits:
@@ -267,26 +530,14 @@
     hi, lo = inverse_factors(diag_blocks)
     if not paired:
         panel_factor, tiles = gathered(slot, panel_blocks, hi, lo, columns)
-        rows = tiles.shape[1]
         keep, send = tiles[: columns // 2], tiles[columns // 2 :].astype(BF16)
-        return (panel_factor, target_tiles - halve_and_add(keep, send, bits, columns, rows)[None])
+        return (panel_factor, target_tiles - halve_and_add(keep, send, bits, columns)[None])
     mine = half.astype(jnp.int32).reshape(1)
     panel_factor, same_keep, same_send, cross_keep, cross_send = panel_products(
         slot, mine, panel_blocks, other, hi, lo, columns
     )
-    rows = panel_blocks.shape[2]
-    same = halve_and_add(same_keep, same_send, bits, columns, rows)
-    diagonal = same[rows : rows + 1] + same[rows + 1 : rows + 2]
-    same = same[:rows] + jnp.where(jnp.eye(rows, dtype=bool), diagonal, 0.0)
-    cross = halve_and_add(cross_keep, cross_send, bits, columns, rows)
-    back = lax.ppermute(cross.astype(BF16), "row", swap)
-    cross = cross + back.astype(F32).T
-    update = jnp.where(
-        half == 0,
-        jnp.concatenate([same, cross], axis=1),
-        jnp.concatenate([cross, same], axis=1),
-    )
-    return (panel_factor, target_tiles - update[None])
+    updated = reduced(bits, same_keep, same_send, cross_keep, cross_send, target_tiles)
+    return (panel_factor, updated)
 
 
 def solution(mesh):

time: 135 us -> 120 us (0.89)
  Pallas kernels: 51.1 us -> 98.5 us
  waiting for transfers between devices: 42.5 us -> 2.68 us
  blocking collectives: 21.8 us -> 0 us
  local copies, waits for them, and re-layouts: 6.53 us -> 13.3 us
  starting transfers between devices: 6.78 us -> 2.94 us
  other arithmetic: 4.42 us -> 0.8 us
    pallas_call x0 -> x2, Pallas kernels: none -> 47.7 us  [the longest x1 38.8 us: reduced(): pl.pallas_call(functools.partial(reduce_kernel, order), out_shape=jax.Sha...]
    ppermute x9 -> x0, waiting for transfers between devices: 42.5 us -> none  [the longest x8 42.5 us: halve_and_add(): got = lax.ppermute(send, 'col', [(c, c ^ 1 << bit) for c in range(columns)])]
    all_gather x1 -> x0, blocking collectives: 21.8 us -> none  [on_device(): lax.all_gather(spread, 'col', axis=0, tiled=True)]
    unnamed x15 -> x19, local copies, waits for them, and re-layouts: 2.02 us -> 7.52 us
    ppermute x9 -> x0, starting transfers between devices: 3.85 us -> none  [the longest x8 2.93 us: halve_and_add(): got = lax.ppermute(send, 'col', [(c, c ^ 1 << bit) for c in range(columns)])]
    ppermute x1, waiting for transfers between devices: 0.01 us -> 2.68 us  [on_device(): other = lax.ppermute(outgoing, 'row', swap)]
    add x9 -> x0, other arithmetic: 2.15 us -> none  [the longest x7 2.12 us: halve_and_add(): value = keep.astype(F32) + got.astype(F32)]
  transfers between devices with their start and end apart: 10 -> 1, of which waited for: 5 -> 1; matrix products, arithmetic and copies ran while one was open for 3% -> 2% of each run, Pallas kernels for 22% -> 32%
where the time goes in v2:
time: 120 us; the launch traced here: 119 us
  Pallas kernels  98.5 us (82%)
  local copies, waits for them, and re-layouts  13.3 us (11%)
  starting transfers between devices  2.94 us (2%)
  waiting for transfers between devices  2.68 us (2%)
  between operations  1.36 us (1%)
    pallas_call x1, Pallas kernels, reduced(): pl.pallas_call(functools.partial(reduce_kernel, order), out_shape=jax.Sha...  38.8 us
    pallas_call x1, Pallas kernels, inverse_factors(): pl.pallas_call(factor_kernel, out_shape=(out, out), in_specs=[pl.BlockSpe...  29.1 us
    pallas_call x1, Pallas kernels, panel_products(): pl.pallas_call(panel_kernel, out_shape=[jax.ShapeDtypeStruct(panel_blocks...  21.7 us
    pallas_call x1, Pallas kernels, ids_by_distance(): pl.pallas_call(ids_kernel, out_shape=jax.ShapeDtypeStruct((columns, 8, 12...  8.91 us
    unnamed x19, local copies, waits for them, and re-layouts  7.52 us
    convert_element_type x1, local copies, waits for them, and re-layouts, on_device(): lax.dynamic_index_in_dim(panel_blocks, 1 - half, 0, keepdims=False)  3.93 us
    ppermute x1, starting transfers between devices, on_device(): other = lax.ppermute(outgoing, 'row', swap)  2.94 us
    ppermute x1, waiting for transfers between devices, on_device(): other = lax.ppermute(outgoing, 'row', swap)  2.68 us
  transfers between devices with their start and end apart: 1, of which 1 were waited for; matrix products, arithmetic and copies ran while one was open for 2% of the time, Pallas kernels for 32%

profile of v2, /device:TPU:0, one launch (start us, length us, event | category | flops | bytes accessed | tf_op | source)
XLA Modules:
  0.0 119.5 jit_solution(603149409902548744)
XLA Ops:
  0.6 0.0 copy-start.8
  0.6 0.0 copy-start.7
  0.7 3.9 %fusion = bf16[8,256,512]{2,1,0:T(8,128)(2,1)} fusion(f32[2,8,256,512]{3,2,1,0:T(8,128)} %panel_ref.1, s32[]{:T(128)S(6)} %select_n.9), kind=kLoop, calls=%fused_computation.1 | loop fusion | bytes 4194308 | tf_op jit(solution)/shard_map/convert_element_type | solution.py:514
  4.6 2.9 %collective-permute-start = (bf16[8,256,512]{2,1,0:T(8,128)(2,1)}, bf16[8,256,512]{2,1,0:T(8,128)(2,1)}, u32[]{:S(2)}, u32[]{:S(2)}) collective-permute-start(bf16[8,256,512]{2,1,0:T(8,128)(2,1)} %fusion), channel_id=1, source_target_pairs={{0,1},{1,0},{2,3},{3,2},{4,5},{5,4},{6,7},{7,6},{8,9},{9,8},{10,11... | collective-permute-start | bytes 6291464 | tf_op jit(solution)/shard_map/ppermute | solution.py:515
  8.2 0.6 broadcast_in_dim.19.own_ref
  8.8 8.9 %ids.1 = s32[16,8,128]{2,1,0:T(8,128)} custom-call(s32[8,128]{1,0:T(8,128)} %broadcast_in_dim.19.own_ref), custom_call_target="tpu_custom_call" | custom-call | tf_op jit(solution)/shard_map/ids/pallas_call | solution.py:287
  17.7 1.2 %slice_reduce_fusion = s32[16]{0:T(128)S(1)} fusion(s32[16,8,128]{2,1,0:T(8,128)} %ids.1), kind=kLoop, calls=%fused_computation.3 | loop fusion | bytes 128 | tf_op jit(solution)/shard_map/slice | solution.py:300
  18.9 0.0 copy-done.8
  18.9 0.2 select_reduce_fusion
  19.1 0.6 and_add_fusion.slot_ref
  19.7 0.0 copy-done.7
  19.7 29.1 %factor.1 = (bf16[2,512,512]{2,1,0:T(8,128)(2,1)S(1)}, bf16[2,512,512]{2,1,0:T(8,128)(2,1)S(1)}) custom-call(f32[2,512,512]{2,1,0:T(8,128)S(1)} %copy-done.7), custom_call_target="tpu_custom_call" | custom-call | flops 40000000000 | bytes 2097152 | tf_op jit(solution)/shard_map/factor/pallas_call | solution.py:100
  48.8 0.0 copy-start
  48.8 1.0 copy-done
  49.8 0.0 copy-start.1
  49.8 1.0 copy-done.1
  50.8 2.7 %collective-permute-done.other_ref = bf16[8,256,512]{2,1,0:T(8,128)(2,1)} collective-permute-done((bf16[8,256,512]{2,1,0:T(8,128)(2,1)}, bf16[8,256,512]{2,1,0:T(8,128)(2,1)}, u32[]{:S(2)}, u32[]{:S(2)}) %collective-permute-start) | collective-permute-done | bytes 2097184 | tf_op jit(solution)/shard_map/ppermute | solution.py:515
  53.5 0.0 copy-start.6
  53.5 21.7 %panel.1 = (f32[2,8,256,512]{3,2,1,0:T(8,128)}, bf16[8,400,128]{2,1,0:T(8,128)(2,1)}, bf16[8,400,128]{2,1,0:T(8,128)(2,1)}, bf16[8,256,256]{2,1,0:T(8,128)(2,1)}, bf16[8,256,256]{2,1,0:T(8,128)(2,1)}) custom-call(s32[2,8]{1,0:T(2,128)} %and_add_fusion.slot_ref, s32[1]{0:T(128)} %bitcast.1.mine_ref, f32[2,8,256,512]{3,2,1,0:T(8,128)} %panel_ref.1, ...), custom_call_target="tpu_custom_call" | custom-call | tf_op jit(solution)/shard_map/panel/pallas_call | solution.py:217
  75.2 0.0 copy-done.6
  75.2 0.0 copy-start.2
  75.2 1.2 %copy-done.2 = bf16[8,256,256]{2,1,0:T(8,128)(2,1)S(1)} copy-done((bf16[8,256,256]{2,1,0:T(8,128)(2,1)S(1)}, bf16[8,256,256]{2,1,0:T(8,128)(2,1)}, u32[]{:S(2)}) %copy-start.2) | copy-done | bytes 1048600
  76.4 0.0 copy-start.3
  76.4 1.2 %copy-done.3 = bf16[8,256,256]{2,1,0:T(8,128)(2,1)S(1)} copy-done((bf16[8,256,256]{2,1,0:T(8,128)(2,1)S(1)}, bf16[8,256,256]{2,1,0:T(8,128)(2,1)}, u32[]{:S(2)}) %copy-start.3) | copy-done | bytes 1048600
  77.6 0.0 copy-start.4
  77.6 1.1 copy-done.4
  78.8 0.0 copy-start.5
  78.8 1.1 copy-done.5
  79.9 38.8 %reduce.3 = f32[1,256,512]{2,1,0:T(8,128)S(1)} custom-call(bf16[8,400,128]{2,1,0:T(8,128)(2,1)S(1)} %copy-done.4, bf16[8,400,128]{2,1,0:T(8,128)(2,1)S(1)} %copy-done.5, bf16[8,256,256]{2,1,0:T(8,128)(2,1)S(1)} %copy-done.2, bf16[8,256,256]{2,1,0:T(8,128)(2,1)S(1)} %copy-done.3, f32[1,256,512]{2,1,0:T(8,128)S(1)} %copy-done.6), custom_call_target="tpu_custom_call" | custom-call | tf_op jit(solution)/shard_map/reduce/pallas_call | solution.py:468
  118.7 0.8 copy.9
Async XLA Ops:
  0.6 18.3 %copy-start.8 = (s32[2,8]{1,0:T(2,128)S(1)}, s32[2,8]{1,0:T(2,128)}, u32[]{:S(2)}) copy-start(s32[2,8]{1,0:T(2,128)} %param.7) | copy-start | bytes 196
  0.6 19.1 %copy-start.7 = (f32[2,512,512]{2,1,0:T(8,128)S(1)}, f32[2,512,512]{2,1,0:T(8,128)}, u32[]{:S(2)}) copy-start(f32[2,512,512]{2,1,0:T(8,128)} %diag_ref.1) | copy-start | bytes 6291460
  4.6 48.9 %collective-permute-start = (bf16[8,256,512]{2,1,0:T(8,128)(2,1)}, bf16[8,256,512]{2,1,0:T(8,128)(2,1)}, u32[]{:S(2)}, u32[]{:S(2)}) collective-permute-start(bf16[8,256,512]{2,1,0:T(8,128)(2,1)} %fusion), channel_id=1, source_target_pairs={{0,1},{1,0},{2,3},{3,2},{4,5},{5,4},{6,7},{7,6},{8,9},{9,8},{10,11... | collective-permute-start | bytes 6291464 | tf_op jit(solution)/shard_map/ppermute | solution.py:515
  48.8 1.0 copy-start
  49.8 1.0 copy-start.1
  53.5 21.7 %copy-start.6 = (f32[1,256,512]{2,1,0:T(8,128)S(1)}, f32[1,256,512]{2,1,0:T(8,128)}, u32[]{:S(2)}) copy-start(f32[1,256,512]{2,1,0:T(8,128)} %target_ref.1) | copy-start | bytes 1572868
  75.2 1.2 %copy-start.2 = (bf16[8,256,256]{2,1,0:T(8,128)(2,1)S(1)}, bf16[8,256,256]{2,1,0:T(8,128)(2,1)}, u32[]{:S(2)}) copy-start(bf16[8,256,256]{2,1,0:T(8,128)(2,1)} %get-tuple-element.14.cross_keep) | copy-start | bytes 3145732
  76.4 1.2 %copy-start.3 = (bf16[8,256,256]{2,1,0:T(8,128)(2,1)S(1)}, bf16[8,256,256]{2,1,0:T(8,128)(2,1)}, u32[]{:S(2)}) copy-start(bf16[8,256,256]{2,1,0:T(8,128)(2,1)} %get-tuple-element.15.cross_send) | copy-start | bytes 3145732
  77.6 1.1 copy-start.4
  78.8 1.1 copy-start.5

commit v3 on v2

--- a/solution.py
+++ b/solution.py
@@ -152,16 +152,24 @@
         for ref in (same_keep, same_send, cross_keep, cross_send):
             ref[...] = jnp.zeros_like(ref)
 
-    def times_inverse(lhs, factor):
-        left = jnp.dot(lhs[:, :low], factor[:low, :low], preferred_element_type=F32)
-        right = jnp.dot(lhs, factor[:, low:], preferred_element_type=F32)
+    def times_inverse(*pairs):
+        left = jnp.dot(
+            jnp.concatenate([lhs[:, :low] for lhs, _ in pairs], axis=1),
+            jnp.concatenate([factor[:low, :low] for _, factor in pairs], axis=0),
+            preferred_element_type=F32,
+        )
+        right = jnp.dot(
+            jnp.concatenate([lhs for lhs, _ in pairs], axis=1),
+            jnp.concatenate([factor[:, low:] for _, factor in pairs], axis=0),
+            preferred_element_type=F32,
+        )
         return jnp.concatenate([left, right], axis=1)
 
     hi, lo = hi_ref[0], lo_ref[0]
     rhs = panel_ref[0].reshape(blocks * rows, width)
     rhs_hi = rhs.astype(BF16)
     rhs_lo = (rhs - rhs_hi.astype(F32)).astype(BF16)
-    solved = times_inverse(rhs_hi, hi) + times_inverse(rhs_lo, hi) + times_inverse(rhs_hi, lo)
+    solved = times_inverse((rhs_hi, hi), (rhs_lo, hi), (rhs_hi, lo))
     out_ref[0] = solved.reshape(blocks, rows, width)
     rounded = solved.astype(BF16).reshape(blocks, rows, width)
     diagonal = lax.broadcasted_iota(jnp.int32, (rows, rows), 0) == lax.broadcasted_iota(
@@ -185,7 +193,7 @@
     @pl.when(s == mine_ref[0])
     def _():
         got = other_ref[...].reshape(blocks * rows, width)
-        partner = (times_inverse(got, hi) + times_inverse(got, lo)).astype(BF16)
+        partner = times_inverse((got, hi), (got, lo)).astype(BF16)
         partner = partner.reshape(blocks, rows, width)
         for i in range(blocks):
             slot = slot_ref[s, j * blocks + i]
@@ -301,7 +309,8 @@
 
 
 def reduce_kernel(
-    order, same_keep, same_send, cross_keep, cross_send, target_ref, out_ref,
+    order, same_held, same_send, cross_held, cross_send, target_ref, out_ref,
+    same_keep, cross_keep, local_sem,
     same_acc, same_out, same_got, cross_acc, cross_out, cross_got0, cross_got,
     swap_out, swap_got, last_out, last_got, full, send_sem, recv_sem,
 ):
@@ -310,6 +319,10 @@
     peers = [(flipped(me, 1 << bit), half) for bit in order]
     stages = len(order)
     rows = 2 * NB
+    cross_load = pltpu.make_async_copy(cross_held, cross_keep, local_sem.at[0])
+    same_load = pltpu.make_async_copy(same_held, same_keep, local_sem.at[1])
+    cross_load.start()
+    same_load.start()
     meet(peers + [partner])
     extra = lax.broadcasted_iota(jnp.int32, (16, NB), 0)
     kept_rows = pl.ds(pl.multiple_of(half * NB, NB), NB)
@@ -415,8 +428,10 @@
 
     cross_copy = remote(stages, cross_send, cross_got0, peers[0])
     same_copy = remote(0, same_send, same_got.at[pl.ds(0, count)], peers[0])
+    cross_load.wait()
     cross_copy.wait()
     swap_copy = cross_first()
+    same_load.wait()
     same_copy.wait()
     same_copy = same_stage(0)
     cross_copy = swap_copy
@@ -468,9 +483,12 @@
     return pl.pallas_call(
         functools.partial(reduce_kernel, order),
         out_shape=jax.ShapeDtypeStruct(target_tiles.shape, F32),
-        in_specs=[vmem] * 5,
+        in_specs=[pl.BlockSpec(memory_space=pl.ANY)] * 4 + [vmem],
         out_specs=vmem,
         scratch_shapes=[
+            pltpu.VMEM(same_keep.shape, BF16),
+            pltpu.VMEM(cross_keep.shape, BF16),
+            pltpu.SemaphoreType.DMA((2,)),
             pltpu.VMEM((count,) + tile, F32),
             pltpu.VMEM((count,) + tile, BF16),
             pltpu.VMEM((2 * count,) + tile, BF16),

time: 120 us -> 120 us (level)
  no operation moved by 1% of the time
where the time goes in v3:
time: 120 us
  Pallas kernels  98.7 us (82%)
  local copies, waits for them, and re-layouts  13.3 us (11%)
  starting transfers between devices  2.94 us (2%)
  waiting for transfers between devices  2.68 us (2%)
  between operations  1.36 us (1%)
    pallas_call x1, Pallas kernels, reduced(): pl.pallas_call(functools.partial(reduce_kernel, order), out_shape=jax.Sha...  39.1 us
    pallas_call x1, Pallas kernels, inverse_factors(): pl.pallas_call(factor_kernel, out_shape=(out, out), in_specs=[pl.BlockSpe...  29.1 us
    pallas_call x1, Pallas kernels, panel_products(): pl.pallas_call(panel_kernel, out_shape=[jax.ShapeDtypeStruct(panel_blocks...  21.7 us
    pallas_call x1, Pallas kernels, ids_by_distance(): pl.pallas_call(ids_kernel, out_shape=jax.ShapeDtypeStruct((columns, 8, 12...  8.91 us
    unnamed x19, local copies, waits for them, and re-layouts  7.52 us
    convert_element_type x1, local copies, waits for them, and re-layouts, on_device(): lax.dynamic_index_in_dim(panel_blocks, 1 - half, 0, keepdims=False)  3.93 us
    ppermute x1, starting transfers between devices, on_device(): other = lax.ppermute(outgoing, 'row', swap)  2.94 us
    ppermute x1, waiting for transfers between devices, on_device(): other = lax.ppermute(outgoing, 'row', swap)  2.68 us
  transfers between devices with their start and end apart: 1, of which 1 were waited for; matrix products, arithmetic and copies ran while one was open for 2% of the time, Pallas kernels for 32%

profile of v3, /device:TPU:0, one launch (start us, length us, event | category | flops | bytes accessed | tf_op | source)
XLA Modules:
  0.0 119.8 jit_solution(12070008713171898752)
XLA Ops:
  0.6 0.0 copy-start.8
  0.6 0.0 copy-start.7
  0.7 3.9 %fusion = bf16[8,256,512]{2,1,0:T(8,128)(2,1)} fusion(f32[2,8,256,512]{3,2,1,0:T(8,128)} %panel_ref.1, s32[]{:T(128)S(6)} %select_n.9), kind=kLoop, calls=%fused_computation.1 | loop fusion | bytes 4194308 | tf_op jit(solution)/shard_map/convert_element_type | solution.py:532
  4.6 2.9 %collective-permute-start = (bf16[8,256,512]{2,1,0:T(8,128)(2,1)}, bf16[8,256,512]{2,1,0:T(8,128)(2,1)}, u32[]{:S(2)}, u32[]{:S(2)}) collective-permute-start(bf16[8,256,512]{2,1,0:T(8,128)(2,1)} %fusion), channel_id=1, source_target_pairs={{0,1},{1,0},{2,3},{3,2},{4,5},{5,4},{6,7},{7,6},{8,9},{9,8},{10,11... | collective-permute-start | bytes 6291464 | tf_op jit(solution)/shard_map/ppermute | solution.py:533
  8.2 0.6 broadcast_in_dim.19.own_ref
  8.8 8.9 %ids.1 = s32[16,8,128]{2,1,0:T(8,128)} custom-call(s32[8,128]{1,0:T(8,128)} %broadcast_in_dim.19.own_ref), custom_call_target="tpu_custom_call" | custom-call | tf_op jit(solution)/shard_map/ids/pallas_call | solution.py:295
  17.7 1.2 %slice_reduce_fusion = s32[16]{0:T(128)S(1)} fusion(s32[16,8,128]{2,1,0:T(8,128)} %ids.1), kind=kLoop, calls=%fused_computation.3 | loop fusion | bytes 128 | tf_op jit(solution)/shard_map/slice | solution.py:308
  18.9 0.0 copy-done.8
  18.9 0.2 select_reduce_fusion
  19.1 0.6 and_add_fusion.slot_ref
  19.7 0.0 copy-done.7
  19.7 29.1 %factor.1 = (bf16[2,512,512]{2,1,0:T(8,128)(2,1)S(1)}, bf16[2,512,512]{2,1,0:T(8,128)(2,1)S(1)}) custom-call(f32[2,512,512]{2,1,0:T(8,128)S(1)} %copy-done.7), custom_call_target="tpu_custom_call" | custom-call | flops 40000000000 | bytes 2097152 | tf_op jit(solution)/shard_map/factor/pallas_call | solution.py:100
  48.8 0.0 copy-start
  48.8 1.0 copy-done
  49.8 0.0 copy-start.1
  49.8 1.0 copy-done.1
  50.8 2.7 %collective-permute-done.other_ref = bf16[8,256,512]{2,1,0:T(8,128)(2,1)} collective-permute-done((bf16[8,256,512]{2,1,0:T(8,128)(2,1)}, bf16[8,256,512]{2,1,0:T(8,128)(2,1)}, u32[]{:S(2)}, u32[]{:S(2)}) %collective-permute-start) | collective-permute-done | bytes 2097184 | tf_op jit(solution)/shard_map/ppermute | solution.py:533
  53.5 0.0 copy-start.6
  53.5 21.7 %panel.1 = (f32[2,8,256,512]{3,2,1,0:T(8,128)}, bf16[8,400,128]{2,1,0:T(8,128)(2,1)}, bf16[8,400,128]{2,1,0:T(8,128)(2,1)}, bf16[8,256,256]{2,1,0:T(8,128)(2,1)}, bf16[8,256,256]{2,1,0:T(8,128)(2,1)}) custom-call(s32[2,8]{1,0:T(2,128)} %and_add_fusion.slot_ref, s32[1]{0:T(128)} %bitcast.1.mine_ref, f32[2,8,256,512]{3,2,1,0:T(8,128)} %panel_ref.1, ...), custom_call_target="tpu_custom_call" | custom-call | tf_op jit(solution)/shard_map/panel/pallas_call | solution.py:225
  75.2 0.0 copy-done.6
  75.2 0.0 copy-start.2
  75.2 1.2 %copy-done.2 = bf16[8,256,256]{2,1,0:T(8,128)(2,1)S(1)} copy-done((bf16[8,256,256]{2,1,0:T(8,128)(2,1)S(1)}, bf16[8,256,256]{2,1,0:T(8,128)(2,1)}, u32[]{:S(2)}) %copy-start.2) | copy-done | bytes 1048600
  76.4 0.0 copy-start.3
  76.4 1.2 %copy-done.3 = bf16[8,256,256]{2,1,0:T(8,128)(2,1)S(1)} copy-done((bf16[8,256,256]{2,1,0:T(8,128)(2,1)S(1)}, bf16[8,256,256]{2,1,0:T(8,128)(2,1)}, u32[]{:S(2)}) %copy-start.3) | copy-done | bytes 1048600
  77.6 0.0 copy-start.4
  77.6 1.1 copy-done.4
  78.8 0.0 copy-start.5
  78.8 1.1 copy-done.5
  79.9 39.1 %reduce.3 = f32[1,256,512]{2,1,0:T(8,128)S(1)} custom-call(bf16[8,400,128]{2,1,0:T(8,128)(2,1)S(1)} %copy-done.4, bf16[8,400,128]{2,1,0:T(8,128)(2,1)S(1)} %copy-done.5, bf16[8,256,256]{2,1,0:T(8,128)(2,1)S(1)} %copy-done.2, bf16[8,256,256]{2,1,0:T(8,128)(2,1)S(1)} %copy-done.3, f32[1,256,512]{2,1,0:T(8,128)S(1)} %copy-done.6), custom_call_target="tpu_custom_call" | custom-call | tf_op jit(solution)/shard_map/reduce/pallas_call | solution.py:483
  119.0 0.8 copy.9
Async XLA Ops:
  0.6 18.3 %copy-start.8 = (s32[2,8]{1,0:T(2,128)S(1)}, s32[2,8]{1,0:T(2,128)}, u32[]{:S(2)}) copy-start(s32[2,8]{1,0:T(2,128)} %param.7) | copy-start | bytes 196
  0.6 19.1 %copy-start.7 = (f32[2,512,512]{2,1,0:T(8,128)S(1)}, f32[2,512,512]{2,1,0:T(8,128)}, u32[]{:S(2)}) copy-start(f32[2,512,512]{2,1,0:T(8,128)} %diag_ref.1) | copy-start | bytes 6291460
  4.6 48.9 %collective-permute-start = (bf16[8,256,512]{2,1,0:T(8,128)(2,1)}, bf16[8,256,512]{2,1,0:T(8,128)(2,1)}, u32[]{:S(2)}, u32[]{:S(2)}) collective-permute-start(bf16[8,256,512]{2,1,0:T(8,128)(2,1)} %fusion), channel_id=1, source_target_pairs={{0,1},{1,0},{2,3},{3,2},{4,5},{5,4},{6,7},{7,6},{8,9},{9,8},{10,11... | collective-permute-start | bytes 6291464 | tf_op jit(solution)/shard_map/ppermute | solution.py:533
  48.8 1.0 copy-start
  49.8 1.0 copy-start.1
  53.5 21.7 %copy-start.6 = (f32[1,256,512]{2,1,0:T(8,128)S(1)}, f32[1,256,512]{2,1,0:T(8,128)}, u32[]{:S(2)}) copy-start(f32[1,256,512]{2,1,0:T(8,128)} %target_ref.1) | copy-start | bytes 1572868
  75.2 1.2 %copy-start.2 = (bf16[8,256,256]{2,1,0:T(8,128)(2,1)S(1)}, bf16[8,256,256]{2,1,0:T(8,128)(2,1)}, u32[]{:S(2)}) copy-start(bf16[8,256,256]{2,1,0:T(8,128)(2,1)} %get-tuple-element.14.cross_held) | copy-start | bytes 3145732
  76.4 1.2 %copy-start.3 = (bf16[8,256,256]{2,1,0:T(8,128)(2,1)S(1)}, bf16[8,256,256]{2,1,0:T(8,128)(2,1)}, u32[]{:S(2)}) copy-start(bf16[8,256,256]{2,1,0:T(8,128)(2,1)} %get-tuple-element.15.cross_send) | copy-start | bytes 3145732
  77.6 1.1 copy-start.4
  78.8 1.1 copy-start.5

commit v4 on v3

--- a/solution.py
+++ b/solution.py
@@ -505,7 +505,7 @@
             pltpu.SemaphoreType.DMA((2 * stages + 2,)),
         ],
         compiler_params=pltpu.CompilerParams(
-            collective_id=1, has_side_effects=True, vmem_limit_bytes=48 * 2**20
+            collective_id=1, has_side_effects=True, vmem_limit_bytes=62 * 2**20
         ),
         name="reduce",
     )(same_keep, same_send, cross_keep, cross_send, target_tiles)

time: 120 us -> 118 us (0.983)
  local copies, waits for them, and re-layouts: 13.3 us -> 9.58 us
  Pallas kernels: 98.7 us -> 100 us
    unnamed x19 -> x9, local copies, waits for them, and re-layouts: 7.52 us -> 3.84 us
    pallas_call x1, Pallas kernels: 39.1 us -> 40.8 us  [reduced(): pl.pallas_call(functools.partial(reduce_kernel, order), out_shape=jax.Sha...]
where the time goes in v4:
time: 118 us
  Pallas kernels  100 us (85%)
  local copies, waits for them, and re-layouts  9.58 us (8%)
  starting transfers between devices  2.94 us (2%)
  waiting for transfers between devices  2.7 us (2%)
  between operations  1.34 us (1%)
    pallas_call x1, Pallas kernels, reduced(): pl.pallas_call(functools.partial(reduce_kernel, order), out_shape=jax.Sha...  40.8 us
    pallas_call x1, Pallas kernels, inverse_factors(): pl.pallas_call(factor_kernel, out_shape=(out, out), in_specs=[pl.BlockSpe...  29.1 us
    pallas_call x1, Pallas kernels, panel_products(): pl.pallas_call(panel_kernel, out_shape=[jax.ShapeDtypeStruct(panel_blocks...  21.5 us
    pallas_call x1, Pallas kernels, ids_by_distance(): pl.pallas_call(ids_kernel, out_shape=jax.ShapeDtypeStruct((columns, 8, 12...  8.91 us
    convert_element_type x1, local copies, waits for them, and re-layouts, on_device(): lax.dynamic_index_in_dim(panel_blocks, 1 - half, 0, keepdims=False)  3.93 us
    unnamed x9, local copies, waits for them, and re-layouts  3.84 us
    ppermute x1, starting transfers between devices, on_device(): other = lax.ppermute(outgoing, 'row', swap)  2.94 us
    ppermute x1, waiting for transfers between devices, on_device(): other = lax.ppermute(outgoing, 'row', swap)  2.7 us
  transfers between devices with their start and end apart: 1, of which 1 were waited for; matrix products, arithmetic and copies ran while one was open for 2% of the time, Pallas kernels for 32%

profile of v4, /device:TPU:0, one launch (start us, length us, event | category | flops | bytes accessed | tf_op | source)
XLA Modules:
  0.0 117.7 jit_solution(9051980791627314686)
XLA Ops:
  0.6 0.0 copy-start.3
  0.6 0.0 copy-start.2
  0.7 3.9 %fusion = bf16[8,256,512]{2,1,0:T(8,128)(2,1)} fusion(f32[2,8,256,512]{3,2,1,0:T(8,128)} %panel_ref.1, s32[]{:T(128)S(6)} %select_n.9), kind=kLoop, calls=%fused_computation.1 | loop fusion | bytes 4194308 | tf_op jit(solution)/shard_map/convert_element_type | solution.py:532
  4.6 2.9 %collective-permute-start = (bf16[8,256,512]{2,1,0:T(8,128)(2,1)}, bf16[8,256,512]{2,1,0:T(8,128)(2,1)}, u32[]{:S(2)}, u32[]{:S(2)}) collective-permute-start(bf16[8,256,512]{2,1,0:T(8,128)(2,1)} %fusion), channel_id=1, source_target_pairs={{0,1},{1,0},{2,3},{3,2},{4,5},{5,4},{6,7},{7,6},{8,9},{9,8},{10,11... | collective-permute-start | bytes 6291464 | tf_op jit(solution)/shard_map/ppermute | solution.py:533
  8.2 0.6 broadcast_in_dim.19.own_ref
  8.8 8.9 %ids.1 = s32[16,8,128]{2,1,0:T(8,128)} custom-call(s32[8,128]{1,0:T(8,128)} %broadcast_in_dim.19.own_ref), custom_call_target="tpu_custom_call" | custom-call | tf_op jit(solution)/shard_map/ids/pallas_call | solution.py:295
  17.7 1.2 %slice_reduce_fusion = s32[16]{0:T(128)S(1)} fusion(s32[16,8,128]{2,1,0:T(8,128)} %ids.1), kind=kLoop, calls=%fused_computation.3 | loop fusion | bytes 128 | tf_op jit(solution)/shard_map/slice | solution.py:308
  18.9 0.0 copy-done.3
  18.9 0.2 select_reduce_fusion
  19.1 0.6 and_add_fusion.slot_ref
  19.7 0.0 copy-done.2
  19.7 29.1 %factor.1 = (bf16[2,512,512]{2,1,0:T(8,128)(2,1)S(1)}, bf16[2,512,512]{2,1,0:T(8,128)(2,1)S(1)}) custom-call(f32[2,512,512]{2,1,0:T(8,128)S(1)} %copy-done.2), custom_call_target="tpu_custom_call" | custom-call | flops 40000000000 | bytes 2097152 | tf_op jit(solution)/shard_map/factor/pallas_call | solution.py:100
  48.8 0.0 copy-start
  48.8 1.0 copy-done
  49.8 0.0 copy-start.1
  49.8 1.0 copy-done.1
  50.8 2.7 %collective-permute-done.other_ref = bf16[8,256,512]{2,1,0:T(8,128)(2,1)} collective-permute-done((bf16[8,256,512]{2,1,0:T(8,128)(2,1)}, bf16[8,256,512]{2,1,0:T(8,128)(2,1)}, u32[]{:S(2)}, u32[]{:S(2)}) %collective-permute-start) | collective-permute-done | bytes 2097184 | tf_op jit(solution)/shard_map/ppermute | solution.py:533
  53.5 21.5 %panel.1 = (f32[2,8,256,512]{3,2,1,0:T(8,128)}, bf16[8,400,128]{2,1,0:T(8,128)(2,1)}, bf16[8,400,128]{2,1,0:T(8,128)(2,1)}, bf16[8,256,256]{2,1,0:T(8,128)(2,1)}, bf16[8,256,256]{2,1,0:T(8,128)(2,1)}) custom-call(s32[2,8]{1,0:T(2,128)} %and_add_fusion.slot_ref, s32[1]{0:T(128)} %bitcast.1.mine_ref, f32[2,8,256,512]{3,2,1,0:T(8,128)} %panel_ref.1, ...), custom_call_target="tpu_custom_call" | custom-call | tf_op jit(solution)/shard_map/panel/pallas_call | solution.py:225
  75.0 40.8 %reduce.3 = f32[1,256,512]{2,1,0:T(8,128)} custom-call(bf16[8,400,128]{2,1,0:T(8,128)(2,1)} %get-tuple-element.12.same_held, bf16[8,400,128]{2,1,0:T(8,128)(2,1)} %get-tuple-element.13.same_send, bf16[8,256,256]{2,1,0:T(8,128)(2,1)} %get-tuple-element.14.cross_held, bf16[8,256,256]{2,1,0:T(8,128)(2,1)} %get-tuple-element.15.cross_send, f32[1,256,512]{2,1,0:T(8,128)} %target_ref.1), custom_call_target="tpu_custom_call" | custom-call | tf_op jit(solution)/shard_map/reduce/pallas_call | solution.py:483
  115.8 1.9 %copy.9 = f32[1,256,512]{2,1,0:T(8,128)} copy(f32[1,256,512]{2,1,0:T(8,128)} %reduce.3) | data formatting | bytes 1048576
Async XLA Ops:
  0.6 18.3 %copy-start.3 = (s32[2,8]{1,0:T(2,128)S(1)}, s32[2,8]{1,0:T(2,128)}, u32[]{:S(2)}) copy-start(s32[2,8]{1,0:T(2,128)} %param.7) | copy-start | bytes 196
  0.6 19.1 %copy-start.2 = (f32[2,512,512]{2,1,0:T(8,128)S(1)}, f32[2,512,512]{2,1,0:T(8,128)}, u32[]{:S(2)}) copy-start(f32[2,512,512]{2,1,0:T(8,128)} %diag_ref.1) | copy-start | bytes 6291460
  4.6 48.9 %collective-permute-start = (bf16[8,256,512]{2,1,0:T(8,128)(2,1)}, bf16[8,256,512]{2,1,0:T(8,128)(2,1)}, u32[]{:S(2)}, u32[]{:S(2)}) collective-permute-start(bf16[8,256,512]{2,1,0:T(8,128)(2,1)} %fusion), channel_id=1, source_target_pairs={{0,1},{1,0},{2,3},{3,2},{4,5},{5,4},{6,7},{7,6},{8,9},{9,8},{10,11... | collective-permute-start | bytes 6291464 | tf_op jit(solution)/shard_map/ppermute | solution.py:533
  48.8 1.0 copy-start
  49.8 1.0 copy-start.1
